TPU v7x, 256 devices: a whole 4x4x8 slice. The times are simulated.
256 devices in a mesh: group: 8 (over z_hi, core), gx: 4 (over x), gy: 8 (over y, z_lo).
Axes of the slice: x: 4, y: 4, z: 8 (z_hi: 4, z_lo: 2; z = z_hi * 2 + z_lo), core: 2. Of those that a mesh axis runs over, the one named last changes fastest.
Arguments:
- start_vectors: float32 [8, 4, 8, 8, 384, 128], P('group', 'gx', 'gy')
- tile_blocks: bfloat16 [8, 4, 8, 8, 4, 384, 384], P('group', 'gx', 'gy')
- block_columns: int32 [8, 4, 8, 8, 4], P('group', 'gx', 'gy'), may hold values from 0 to 11, as said below
- sleeve_rod: int32 [4, 8, 7, 8, 8], P('gx', 'gy'), may hold values from -1 to 511, as said below
- sleeve_membrane: int32 [4, 8, 7, 8, 8], P('gx', None, None, 'gy'), may hold values from -1 to 511, as said below
- sleeve_stiffness: float32 [4, 8, 7, 8, 8], P('gx', None, None, 'gy'), may hold values from 0.25 to 4
Outputs:
- final_vectors: float32 [8, 4, 8, 8, 384, 128], P('group', 'gx', 'gy')
- norms: float32 [3, 128], replicated
Inputs may be any that keep to these rules, and one draw needn't show every extreme that they name: `block_columns`: entry 0 of block row r is r itself; every other entry names one of the device's 8 blocks, or 8 to 11 for the west, east, south and north ghost blocks. sleeve_rod[x, y, m, y2, :] lists the nodes of rod device (0, x, y) tied to membrane tile (m + 1, x, y2); -1 marks an empty slot and live slots come first. In every draw one membrane tile receives 8 live slots from each of the 8 rod devices of its column. `sleeve_membrane`: -1 at exactly the slots where sleeve_rod is -1; elsewhere a node of membrane tile (m + 1, x, y2).
All inputs are finite; a program needn't handle non-finite values.
Results may differ from a plain program's by a relative error of at most 0.005.
Values may be sent and summed in bfloat16 or wider, within the bound.
No kernel may reach another device: no remote copies, remote signals or barrier semaphores. Data moves between devices by JAX's collectives and lax.ppermute only.
A program may use at most 64 MiB of HBM per device.

v0:
```python
import functools

import jax
import jax.numpy as jnp
from jax import lax
from jax.experimental import pallas as pl
from jax.experimental.pallas import tpu as pltpu
from jax.sharding import Mesh, PartitionSpec as P

MATVECS = 3
TILE = 384
NB = 8
KB = 4
S = 128
CAP = 8
DOFS = 6
NODES = NB * TILE // DOFS
ROWS = NB * TILE
GROUPS = 8
MEMB = GROUPS - 1
GX_N = 4
GY_N = 8
DEVICES = GROUPS * GX_N * GY_N
SLOTS = MEMB * GY_N * CAP
MSLOTS = GY_N * CAP
MESSAGE = DOFS * CAP
EPS = 1e-06
ALL_DOFS = DEVICES * ROWS
LOWEST, HIGHEST = 1e-20, 1e20

GROUP = ("zh", "core")
GY = ("y", "zl")
AXES = ("zh", "core", "gx", "y", "zl")
PAIRS = GROUPS // 2

VMEM = pl.BlockSpec(memory_space=pltpu.VMEM)
SMEM = pl.BlockSpec(memory_space=pltpu.SMEM)
HBM = pl.BlockSpec(memory_space=pltpu.HBM)
BF16 = jnp.bfloat16
F32 = jnp.float32
VMEM_BYTES = 20 * 1024 * 1024


def dot(a, b):
    return jnp.dot(a, b, preferred_element_type=F32)


def update_kernel(turn, scaled, *refs):
    refs = list(refs)
    take = lambda n: [refs.pop(0) for _ in range(n)]
    first, last = turn == 0, turn == MATVECS
    (flags, base) = take(2)
    if first:
        (gather,) = take(1)
    else:
        (received, handed, own_a, own_b, kappa_in, scatter) = take(6)
        if not last:
            (gather,) = take(1)
        if turn == 1:
            (stiff_message,) = take(1)
        if scaled:
            (inverse,) = take(1)
    if last:
        (y,) = take(1)
    else:
        (rounded_out, x_even, x_odd, y_even, y_odd, send_a, send_b, own_a_out, own_b_out) = take(9)
    if not first:
        (squares,) = take(1)
    kappa = None
    if turn == 1:
        (kappa,) = take(1)
    elif not first:
        kappa = kappa_in
    if scaled:
        (y,) = take(1)
    (slots,) = take(1)
    if not last:
        (rounded, copied) = take(2)
    if not first and not last and not scaled:
        (y,) = take(1)
    is_rod = flags[0] == 0

    def on_rod(f):
        pl.when(is_rod)(f)

    def on_membrane(f):
        pl.when(jnp.logical_not(is_rod))(f)

    if not first:

        def difference(q, mine, theirs):
            gap = mine[...].astype(F32) - theirs[...].astype(F32)
            stiff = kappa[q * MSLOTS : (q + 1) * MSLOTS].reshape(GY_N, 1, CAP, S)
            slots[q * GY_N : (q + 1) * GY_N] = gap.reshape(GY_N, DOFS, CAP, S) * stiff

        @on_rod
        def _():
            if turn == 1:
                parts = stiff_message[...].astype(F32)
                lane = lax.broadcasted_iota(jnp.int32, parts.shape, 2)
                low = jnp.sum(jnp.where(lane < 3, parts, 0.0), axis=2, keepdims=True)
                high = jnp.sum(
                    jnp.where((lane >= 3) & (lane < 6), parts, 0.0)[:, :CAP], axis=2, keepdims=True
                )
                for q in range(MEMB):
                    value = low[:, q * CAP : (q + 1) * CAP] if q < DOFS else high
                    kappa[q * MSLOTS : (q + 1) * MSLOTS] = jnp.broadcast_to(
                        value, (GY_N, CAP, S)
                    ).reshape(MSLOTS, S)
            difference(0, own_b.at[0], received.at[0])
            for q in range(1, PAIRS):
                difference(2 * q - 1, own_a.at[q], received.at[q])
                difference(2 * q, own_b.at[q], handed.at[q])

        @on_membrane
        def _():
            if turn == 1:
                kappa[...] = kappa_in[...]
            difference(0, own_a.at[0], received.at[0])
            slots[GY_N : 2 * GY_N] = jnp.zeros((GY_N, DOFS, CAP, S), F32)

        def pair_of(count, d):
            return jnp.concatenate(
                [slots[:count, d].reshape(count * CAP, S), slots[:count, d + 1].reshape(count * CAP, S)],
                axis=1,
            )

        def finish(d, coupling):
            value = base[pl.ds(d, NODES, stride=DOFS), :] + coupling
            if scaled:
                value = value * inverse[...]
            y[pl.ds(d, NODES, stride=DOFS), :] = value
            return jnp.sum(jnp.square(value).reshape(NODES // 8, 8, S), axis=0)

        @on_rod
        def _():
            total = jnp.zeros((8, S), F32)
            for d in range(0, DOFS, 2):
                coupling = dot(scatter[...], pair_of(MEMB * GY_N, d).astype(BF16))
                total += finish(d, coupling[:, :S]) + finish(d + 1, coupling[:, S:])
            squares[...] = jnp.sum(total, axis=0, keepdims=True)

        @on_membrane
        def _():
            total = jnp.zeros((8, S), F32)
            place = scatter[:, : 2 * MSLOTS]
            for d in range(0, DOFS, 2):
                delta = pair_of(2 * GY_N, d)
                high = delta.astype(BF16)
                low = (delta - high.astype(F32)).astype(BF16)
                coupling = dot(place, high) + dot(place, low)
                total += finish(d, coupling[:, :S]) + finish(d + 1, coupling[:, S:])
            squares[...] = jnp.sum(total, axis=0, keepdims=True)

    if not last:
        source = base if first else y

        for r in range(NB):
            rounded[r] = source[r * TILE : (r + 1) * TILE].astype(BF16)
        copies = [pltpu.make_async_copy(rounded, rounded_out, copied.at[0])]
        copies[0].start()
        odd_x, odd_y = flags[1], flags[2]
        x_even[...] = rounded[(NB - 1) * (1 - odd_x)]
        x_odd[...] = rounded[(NB - 1) * odd_x]
        y_even[...] = rounded[1 + (NB - 3) * odd_y]
        y_odd[...] = rounded[NB - 2 - (NB - 3) * odd_y]

        def collect(count):
            pick = gather[: count * MSLOTS]
            for d in range(0, DOFS, 2):
                values = jnp.concatenate(
                    [source[pl.ds(d + e, NODES, stride=DOFS), :].astype(BF16) for e in range(2)],
                    axis=1,
                )
                rows = dot(pick, values)
                for e in range(2):
                    slots[: count * GY_N, d + e] = rows[:, e * S : (e + 1) * S].reshape(
                        count * GY_N, CAP, S
                    )

        def message(q):
            return slots[q * GY_N : (q + 1) * GY_N].reshape(GY_N, MESSAGE, S).astype(BF16)

        nothing = jnp.zeros((GY_N, MESSAGE, S), BF16)

        @on_rod
        def _():
            collect(MEMB)
            send_a[0] = nothing
            send_b[0] = message(0)
            for q in range(1, PAIRS):
                send_a[q] = message(2 * q - 1)
                send_b[q] = message(2 * q)

        @on_membrane
        def _():
            collect(1)
            send_a[0] = message(0)
            send_b[0] = message(0)
            for q in range(1, PAIRS):
                send_a[q] = nothing
                send_b[q] = nothing

        copies.append(pltpu.make_async_copy(send_a, own_a_out, copied.at[1]))
        copies.append(pltpu.make_async_copy(send_b, own_b_out, copied.at[2]))
        for copy in copies[1:]:
            copy.start()
        for copy in copies:
            copy.wait()


def update(turn, scaled, args):
    first, last = turn == 0, turn == MATVECS
    if last:
        out = [jax.ShapeDtypeStruct((ROWS, S), F32)]
    else:
        out = [pltpu.HBM((NB, TILE, S), BF16)]
        out += [jax.ShapeDtypeStruct((TILE, S), BF16)] * 4
        out += [jax.ShapeDtypeStruct((PAIRS, GY_N, MESSAGE, S), BF16)] * 2
        out += [pltpu.HBM((PAIRS, GY_N, MESSAGE, S), BF16)] * 2
    if not first:
        out += [jax.ShapeDtypeStruct((1, S), F32)]
    if turn == 1:
        out += [jax.ShapeDtypeStruct((SLOTS, S), F32)]
    if scaled:
        out += [jax.ShapeDtypeStruct((ROWS, S), F32)]
    specs = [VMEM] * len(out)
    scratch = [pltpu.VMEM((MEMB * GY_N, DOFS, CAP, S), F32)]
    if not last:
        specs[0] = specs[7] = specs[8] = HBM
        scratch += [pltpu.VMEM((NB, TILE, S), BF16), pltpu.SemaphoreType.DMA((3,))]
    if not first and not last and not scaled:
        scratch += [pltpu.VMEM((ROWS, S), F32)]
    return pl.pallas_call(
        functools.partial(update_kernel, turn, scaled),
        out_shape=out,
        in_specs=[SMEM] + [VMEM] * (len(args) - 1),
        out_specs=specs,
        scratch_shapes=scratch,
        compiler_params=pltpu.CompilerParams(vmem_limit_bytes=VMEM_BYTES),
        name="update",
    )(*args)


def inner_kernel(columns, blocks, rounded, out, token, extended, copied):
    copy = pltpu.make_async_copy(rounded, extended.at[:NB], copied)
    copy.start()
    extended[NB] = jnp.zeros((TILE, S), BF16)
    copy.wait()

    def row_of(r, _):
        row = jnp.concatenate([blocks[r, k] for k in range(KB)], axis=1)
        picked = jnp.concatenate(
            [extended[jnp.minimum(columns[r, k], NB)] for k in range(KB)], axis=0
        )
        out[pl.ds(pl.multiple_of(r * TILE, TILE), TILE)] = dot(row, picked)
        return 0

    lax.fori_loop(0, NB, row_of, 0, unroll=4)
    token[...] = out[:8]


def inner(columns, blocks, rounded):
    return pl.pallas_call(
        inner_kernel,
        out_shape=[jax.ShapeDtypeStruct((ROWS, S), F32), jax.ShapeDtypeStruct((8, S), F32)],
        in_specs=[SMEM, VMEM, HBM],
        out_specs=[VMEM, VMEM],
        scratch_shapes=[pltpu.VMEM((NB + 1, TILE, S), BF16), pltpu.SemaphoreType.DMA],
        compiler_params=pltpu.CompilerParams(vmem_limit_bytes=VMEM_BYTES),
        cost_estimate=pl.CostEstimate(
            flops=2 * NB * KB * TILE * TILE * S, bytes_accessed=12_000_000, transcendentals=0
        ),
        name="inner",
    )(columns, blocks, rounded)


def outer_kernel(columns, flags, blocks, base, x_even, x_odd, y_even, y_odd, out, edges, tiles, copied):
    def copy_of(r, k):
        j = r * (KB - 1) + k - 1
        return pltpu.make_async_copy(blocks.at[r, k], tiles.at[j], copied.at[j])

    def fetch(r, _):
        for k in range(1, KB):
            pl.when(columns[r, k] >= NB)(copy_of(r, k).start)
        return 0

    lax.fori_loop(0, NB, fetch, 0)
    odd_x, odd_y = flags[1], flags[2]
    edges[1 - odd_x] = x_even[...]
    edges[odd_x] = x_odd[...]
    edges[3 - odd_y] = y_even[...]
    edges[2 + odd_y] = y_odd[...]

    def add(r, _):
        rows = pl.ds(pl.multiple_of(r * TILE, TILE), TILE)
        out[rows] = base[rows]
        for k in range(1, KB):

            @pl.when(columns[r, k] >= NB)
            def _():
                copy_of(r, k).wait()
                out[rows] += dot(tiles[r * (KB - 1) + k - 1], edges[columns[r, k] - NB])

        return 0

    lax.fori_loop(0, NB, add, 0)


def outer(columns, flags, blocks, base, halo):
    count = NB * (KB - 1)
    return pl.pallas_call(
        outer_kernel,
        out_shape=jax.ShapeDtypeStruct((ROWS, S), F32),
        in_specs=[SMEM, SMEM, HBM] + [VMEM] * 5,
        out_specs=VMEM,
        scratch_shapes=[
            pltpu.VMEM((4, TILE, S), BF16),
            pltpu.VMEM((count, TILE, TILE), BF16),
            pltpu.SemaphoreType.DMA((count,)),
        ],
        compiler_params=pltpu.CompilerParams(vmem_limit_bytes=VMEM_BYTES),
        cost_estimate=pl.CostEstimate(
            flops=8 * 2 * TILE * TILE * S, bytes_accessed=6_000_000, transcendentals=0
        ),
        name="outer",
    )(columns, flags, blocks, base, *halo)


def swaps(count, start):
    pairs = []
    for i in range(start, count - 1, 2):
        pairs += [(i, i + 1), (i + 1, i)]
    return pairs


def halos(edges):
    (x_even, x_odd, y_even, y_odd) = edges
    return (
        lax.ppermute(x_even, "gx", swaps(GX_N, 0)),
        lax.ppermute(x_odd, "gx", swaps(GX_N, 1)),
        lax.ppermute(y_even, GY, swaps(GY_N, 0)),
        lax.ppermute(y_odd, GY, swaps(GY_N, 1)),
    )


def total_of(rows):
    total = rows.reshape(1, -1)
    for axes, count in ((("gx", "y"), 16), (("zh", "core", "zl"), 16)):
        spread = jnp.broadcast_to(total, (count, total.shape[1]))
        gathered = lax.all_to_all(spread, axes, split_axis=0, concat_axis=0, tiled=True)
        total = jnp.sum(gathered, axis=0, keepdims=True)
    return total.reshape(rows.shape)


def merge(group, own, passed, extra):
    block = jnp.arange(PAIRS)
    relay = (group == 1) | ((group == 0) & (block == 0))
    send = jnp.where(relay[:, None, None, None], passed, own)
    if extra is not None:
        free = (group > 1) & (block == 1)
        send = jnp.where(free[:, None, None, None], extra[None], send)
    return send


def exchange(send):
    return lax.all_to_all(
        send.reshape(PAIRS * GY_N, MESSAGE, S),
        ("zh", "y", "zl"),
        split_axis=0,
        concat_axis=0,
        tiled=True,
    ).reshape(PAIRS, GY_N, MESSAGE, S)


def after_kernel(value, *refs):
    refs[-1][...] = value[...]


def after(value, tokens):
    return pl.pallas_call(
        after_kernel,
        out_shape=jax.ShapeDtypeStruct(value.shape, value.dtype),
        in_specs=[VMEM] * (1 + len(tokens)),
        out_specs=VMEM,
        compiler_params=pltpu.CompilerParams(vmem_limit_bytes=VMEM_BYTES),
        name="after",
    )(value, *tokens)


def split(values):
    high = lax.reduce_precision(values, 8, 7)
    middle = lax.reduce_precision(values - high, 8, 7)
    return jnp.stack([high, middle, values - high - middle], axis=-1).astype(BF16)


def local(start_vectors, tile_blocks, block_columns, sleeve_rod, sleeve_membrane, sleeve_stiffness):
    group = lax.axis_index(GROUP)
    is_rod = group == 0
    memb = jnp.maximum(group - 1, 0)
    blocks = tile_blocks[0, 0, 0]
    columns = block_columns[0, 0, 0]
    odd_x = lax.axis_index("gx") % 2
    odd_y = lax.axis_index("zl")
    flags = jnp.stack([group, odd_x, odd_y])

    rod_nodes = sleeve_rod[0, 0].reshape(SLOTS)
    memb_nodes = lax.dynamic_index_in_dim(
        sleeve_membrane[0, :, :, 0, :], memb, axis=1, keepdims=False
    ).reshape(MSLOTS)
    rest = SLOTS - MSLOTS
    memb_nodes = jnp.concatenate([memb_nodes, jnp.full((rest,), -1, jnp.int32)])
    nodes = jnp.where(is_rod, rod_nodes, memb_nodes)
    ids = jnp.arange(NODES, dtype=jnp.int32)
    gather = (nodes[:, None] == ids[None, :]).astype(BF16)
    scatter = (ids[:, None] == nodes[None, :]).astype(BF16)

    stiff = sleeve_stiffness[0, :, :, 0, :]
    pieces = split(stiff)
    low = pieces[:, :DOFS].reshape(GY_N, MESSAGE, 3)
    high = jnp.pad(pieces[:, DOFS], ((0, 0), (0, MESSAGE - CAP), (0, 0)))
    stiff_message = jnp.pad(jnp.concatenate([low, high], axis=2), ((0, 0), (0, 0), (0, S - 6)))
    kappa = lax.dynamic_index_in_dim(stiff, memb, axis=1, keepdims=False).reshape(MSLOTS)
    kappa = jnp.concatenate([kappa, jnp.zeros((rest,), F32)])
    kappa = jnp.broadcast_to(kappa[:, None], (SLOTS, S))
    start = start_vectors[0, 0, 0].reshape(ROWS, S)

    def step(turn, state, kappa, inverse=None):
        (rounded, *edges, send_a, send_b, own_a, own_b) = state[:9]
        passed = lax.ppermute(send_b, GROUP, [(0, 1), (1, 0)])
        received = exchange(merge(group, send_a, passed, stiff_message if turn == 1 else None))
        halo = halos(edges)
        (part, token) = inner(columns, blocks, rounded)
        received = after(received, [token, *halo])
        handed = lax.ppermute(received, GROUP, [(1, 0)])
        base = outer(columns, flags, blocks, part, halo)
        args = [flags, base, received, handed, own_a, own_b, kappa, scatter]
        if turn < MATVECS:
            args += [gather]
        if turn == 1:
            args += [lax.ppermute(received[1], GROUP, [(2, 0)])]
        if inverse is not None:
            args += [inverse]
        return update(turn, inverse is not None, args)

    begun = update(0, False, [flags, start, gather])
    once = step(1, begun, kappa)
    kappa = once[10]
    twice = step(2, once, kappa)
    (value, last) = step(3, twice, kappa)

    sums = total_of(jnp.concatenate([once[9], twice[9], last], axis=0)) / ALL_DOFS
    safe = jnp.all((sums > LOWEST) & (sums < HIGHEST))
    first_norm = jnp.sqrt(sums[0:1] + EPS)

    def quick(_):
        second_norm = jnp.sqrt(sums[1:2] / jnp.square(first_norm) + EPS)
        both = first_norm * second_norm
        third_norm = jnp.sqrt(sums[2:3] / jnp.square(both) + EPS)
        final = value * (1.0 / (both * third_norm))
        return (final, jnp.concatenate([first_norm, second_norm, third_norm], axis=0))

    def careful(_):
        def turn(k, carry):
            (state, norm, norms, _) = carry
            (*state, squares, value) = step(2, state, kappa, 1.0 / norm)
            norm = jnp.sqrt(total_of(squares) / ALL_DOFS + EPS)
            return (state, norm, norms.at[k].set(norm[0]), value)

        state = update(0, False, [flags, start, gather])
        zero = jnp.zeros((MATVECS, S), F32)
        carry = (list(state), jnp.ones((1, S), F32), zero, jnp.zeros((ROWS, S), F32))
        (_, norm, norms, value) = lax.fori_loop(0, MATVECS, turn, carry)
        return (value / norm, norms)

    (final, norms) = lax.cond(safe, quick, careful, None)
    return (final.reshape(1, 1, 1, NB, TILE, S), norms)


def solution(mesh):
    fine = Mesh(mesh.devices.reshape(4, 2, GX_N, 4, 2), AXES)
    spread = (GROUP, "gx", GY)
    return jax.shard_map(
        local,
        mesh=fine,
        in_specs=(
            P(*spread, None, None, None),
            P(*spread, None, None, None, None),
            P(*spread, None, None),
            P("gx", GY, None, None, None),
            P("gx", None, None, GY, None),
            P("gx", None, None, GY, None),
        ),
        out_specs=(P(*spread, None, None, None), P()),
        check_vma=False,
    )
```

profile of v0, /device:TPU:1, one launch (start us, length us, event | category | flops | bytes accessed | tf_op | source)
XLA Modules:
  0.0 151.6 jit_solution(12382165820826918744)
XLA Ops:
  2.6 3.5 %update.13 = (bf16[8,384,128]{2,1,0:T(8,128)(2,1)}, bf16[384,128]{1,0:T(8,128)(2,1)}, bf16[384,128]{1,0:T(8,128)(2,1)}, bf16[384,128]{1,0:T(8,128)(2,1)}, bf16[3...) custom-call(s32[3]{0:T(128)S(1)} %pad_add_fusion.refs_0_.flags, ...), custom_call_target="tpu_custom_call" | custom-call | tf_op jit(solution)/shard_map/update/pallas_call | solution.py:234
  6.1 5.5 %collective-permute-start.10 = (bf16[4,8,48,128]{3,2,1,0:T(8,128)(2,1)S(1)}, bf16[4,8,48,128]{3,2,1,0:T(8,128)(2,1)S(1)}, u32[]{:S(2)}, u32[]{:S(2)}) collective-permute-start(bf16[4,8,48,128]{3,2,1,0:T(8,128)(2,1)S(1)} %get-tuple-element.595), channel_id=1, source_target_pairs={{0,32},{32,0},{1,33},{33,1},{2,34},{34,2},{3,35},{35,3},{4,36},{36... | collective-permute-start | bytes 1179656 | tf_op jit(solution)/shard_map/ppermute | solution.py:430
  13.8 6.4 %all-to-all-start.3 = ((bf16[32,48,128]{2,1,0:T(8,128)(2,1)}), bf16[32,48,128]{2,1,0:T(8,128)(2,1)S(1)}, u32[]{:S(2)}, u32[]{:S(2)}) async-start(bf16[32,48,128]{2,1,0:T(8,128)(2,1)} %bitcast.22), calls=%async_computation.3 | async-start | bytes 786432 | tf_op jit(solution)/shard_map/all_to_all | solution.py:367
  22.2 1.3 collective-permute-start.8
  24.3 6.5 %inner.10 = (f32[3072,128]{1,0:T(8,128)S(1)}, f32[8,128]{1,0:T(8,128)S(1)}) custom-call(s32[8,4]{1,0:T(8,128)S(1)} %copy.40.columns, bf16[8,4,384,384]{3,2,1,0:T(8,128)(2,1)} %bitcast.80, bf16[8,384,128]{2,1,0:T(8,128)(2,1)S(1)} %copy-done.1), custom_call_target="tpu_custom_call" | custom-call | flops 1207959552 | bytes 12000000 | tf_op jit(solution)/shard_map/inner/pallas_call | solution.py:264
  34.1 5.9 %collective-permute-start.11 = (bf16[4,8,48,128]{3,2,1,0:T(8,128)(2,1)S(1)}, bf16[4,8,48,128]{3,2,1,0:T(8,128)(2,1)}, u32[]{:S(2)}, u32[]{:S(2)}) collective-permute-start(bf16[4,8,48,128]{3,2,1,0:T(8,128)(2,1)S(1)} %after.4.refs_2_), channel_id=1, source_target_pairs={{32,0},{33,1},{34,2},{35,3},{36,4},{37,5},{38,6},{39,7},{40,8},{41... | collective-permute-start | bytes 1179656 | tf_op jit(solution)/shard_map/ppermute | solution.py:435
  41.8 5.0 %outer.4.refs_1_ = f32[3072,128]{1,0:T(8,128)S(1)} custom-call(s32[8,4]{1,0:T(8,128)S(1)} %copy.40.columns, s32[3]{0:T(128)S(1)} %pad_add_fusion.refs_0_.flags, bf16[8,4,384,384]{3,2,1,0:T(8,128)(2,1)} %bitcast.81, f32[3072,128]{1,0:T(8,128)S(1)} %get-tuple-element.590.base, bf16[384,128]{1,0:T(8,128)(2,1)S(1)} %collective-permute-done.6.x_even.refs_1_, ...), custom_call_target="tpu_custom_call" | custom-call | flops 301989888 | bytes 6000000 | tf_op jit(solution)/shard_map/outer/pallas_call | solution.py:312
  46.9 3.7 %update.14 = (bf16[8,384,128]{2,1,0:T(8,128)(2,1)}, bf16[384,128]{1,0:T(8,128)(2,1)}, bf16[384,128]{1,0:T(8,128)(2,1)}, bf16[384,128]{1,0:T(8,128)(2,1)S(1)}, bf...) custom-call(s32[3]{0:T(128)S(1)} %pad_add_fusion.refs_0_.flags, ...), custom_call_target="tpu_custom_call" | custom-call | tf_op jit(solution)/shard_map/update/pallas_call | solution.py:234
  50.6 2.1 %collective-permute-start.17 = (bf16[4,8,48,128]{3,2,1,0:T(8,128)(2,1)S(1)}, bf16[4,8,48,128]{3,2,1,0:T(8,128)(2,1)S(1)}, u32[]{:S(2)}, u32[]{:S(2)}) collective-permute-start(bf16[4,8,48,128]{3,2,1,0:T(8,128)(2,1)S(1)} %get-tuple-element.607), channel_id=1, source_target_pairs={{0,32},{32,0},{1,33},{33,1},{2,34},{34,2},{3,35},{35,3},{4,36},{36... | collective-permute-start | bytes 1179656 | tf_op jit(solution)/shard_map/ppermute | solution.py:430
  52.7 1.7 %collective-permute-done.17 = bf16[4,8,48,128]{3,2,1,0:T(8,128)(2,1)S(1)} collective-permute-done((bf16[4,8,48,128]{3,2,1,0:T(8,128)(2,1)S(1)}, bf16[4,8,48,128]{3,2,1,0:T(8,128)(2,1)S(1)}, u32[]{:S(2)}, u32[]{:S(2)}) %collective-permute-start.17) | collective-permute-done | bytes 393248 | tf_op jit(solution)/shard_map/ppermute | solution.py:430
  55.3 4.9 %all-to-all-start.4 = ((bf16[32,48,128]{2,1,0:T(8,128)(2,1)}), bf16[32,48,128]{2,1,0:T(8,128)(2,1)S(1)}, u32[]{:S(2)}, u32[]{:S(2)}) async-start(bf16[32,48,128]{2,1,0:T(8,128)(2,1)} %bitcast.25), calls=%async_computation.4 | async-start | bytes 786432 | tf_op jit(solution)/shard_map/all_to_all | solution.py:367
  60.1 2.8 %collective-permute-start.13 = (bf16[384,128]{1,0:T(8,128)(2,1)}, bf16[384,128]{1,0:T(8,128)(2,1)S(1)}, u32[]{:S(2)}, u32[]{:S(2)}) collective-permute-start(bf16[384,128]{1,0:T(8,128)(2,1)} %get-tuple-element.603), channel_id=1, source_target_pairs={{0,8},{8,0},{16,24},{24,16},{1,9},{9,1},{17,25},{25,17},{2,10},{10... | collective-permute-start | bytes 294920 | tf_op jit(solution)/shard_map/ppermute | solution.py:340
  63.6 1.3 collective-permute-start.15
  65.6 6.5 %inner.11 = (f32[3072,128]{1,0:T(8,128)S(1)}, f32[8,128]{1,0:T(8,128)S(1)}) custom-call(s32[8,4]{1,0:T(8,128)S(1)} %copy.40.columns, bf16[8,4,384,384]{3,2,1,0:T(8,128)(2,1)} %bitcast.82, bf16[8,384,128]{2,1,0:T(8,128)(2,1)S(1)} %copy-done.2), custom_call_target="tpu_custom_call" | custom-call | flops 1207959552 | bytes 12000000 | tf_op jit(solution)/shard_map/inner/pallas_call | solution.py:264
  73.2 4.9 %collective-permute-start.18 = (bf16[4,8,48,128]{3,2,1,0:T(8,128)(2,1)S(1)}, bf16[4,8,48,128]{3,2,1,0:T(8,128)(2,1)S(1)}, u32[]{:S(2)}, u32[]{:S(2)}) collective-permute-start(bf16[4,8,48,128]{3,2,1,0:T(8,128)(2,1)S(1)} %after.5.refs_2_), channel_id=1, source_target_pairs={{32,0},{33,1},{34,2},{35,3},{36,4},{37,5},{38,6},{39,7},{40,8},{41... | collective-permute-start | bytes 1179656 | tf_op jit(solution)/shard_map/ppermute | solution.py:435
  78.2 5.0 %outer.5.refs_1_ = f32[3072,128]{1,0:T(8,128)S(1)} custom-call(s32[8,4]{1,0:T(8,128)S(1)} %copy.40.columns, s32[3]{0:T(128)S(1)} %pad_add_fusion.refs_0_.flags, bf16[8,4,384,384]{3,2,1,0:T(8,128)(2,1)} %bitcast.83, f32[3072,128]{1,0:T(8,128)S(1)} %get-tuple-element.602.base, bf16[384,128]{1,0:T(8,128)(2,1)S(1)} %collective-permute-done.13.x_even.refs_1_, ...), custom_call_target="tpu_custom_call" | custom-call | flops 301989888 | bytes 6000000 | tf_op jit(solution)/shard_map/outer/pallas_call | solution.py:312
  83.2 3.3 %update.15 = (bf16[8,384,128]{2,1,0:T(8,128)(2,1)}, bf16[384,128]{1,0:T(8,128)(2,1)}, bf16[384,128]{1,0:T(8,128)(2,1)}, bf16[384,128]{1,0:T(8,128)(2,1)S(1)}, bf...) custom-call(s32[3]{0:T(128)S(1)} %pad_add_fusion.refs_0_.flags, ...), custom_call_target="tpu_custom_call" | custom-call | tf_op jit(solution)/shard_map/update/pallas_call | solution.py:234
  86.5 2.1 %collective-permute-start.23 = (bf16[4,8,48,128]{3,2,1,0:T(8,128)(2,1)S(1)}, bf16[4,8,48,128]{3,2,1,0:T(8,128)(2,1)S(1)}, u32[]{:S(2)}, u32[]{:S(2)}) collective-permute-start(bf16[4,8,48,128]{3,2,1,0:T(8,128)(2,1)S(1)} %get-tuple-element.620), channel_id=1, source_target_pairs={{0,32},{32,0},{1,33},{33,1},{2,34},{34,2},{3,35},{35,3},{4,36},{36... | collective-permute-start | bytes 1179656 | tf_op jit(solution)/shard_map/ppermute | solution.py:430
  88.6 1.7 %collective-permute-done.23 = bf16[4,8,48,128]{3,2,1,0:T(8,128)(2,1)S(1)} collective-permute-done((bf16[4,8,48,128]{3,2,1,0:T(8,128)(2,1)S(1)}, bf16[4,8,48,128]{3,2,1,0:T(8,128)(2,1)S(1)}, u32[]{:S(2)}, u32[]{:S(2)}) %collective-permute-start.23) | collective-permute-done | bytes 393248 | tf_op jit(solution)/shard_map/ppermute | solution.py:430
  91.1 4.7 %all-to-all-start.5 = ((bf16[32,48,128]{2,1,0:T(8,128)(2,1)}), bf16[32,48,128]{2,1,0:T(8,128)(2,1)S(1)}, u32[]{:S(2)}, u32[]{:S(2)}) async-start(bf16[32,48,128]{2,1,0:T(8,128)(2,1)} %bitcast.27), calls=%async_computation.5 | async-start | bytes 786432 | tf_op jit(solution)/shard_map/all_to_all | solution.py:367
  95.9 2.3 %collective-permute-start.19 = (bf16[384,128]{1,0:T(8,128)(2,1)}, bf16[384,128]{1,0:T(8,128)(2,1)S(1)}, u32[]{:S(2)}, u32[]{:S(2)}) collective-permute-start(bf16[384,128]{1,0:T(8,128)(2,1)} %get-tuple-element.616), channel_id=1, source_target_pairs={{0,8},{8,0},{16,24},{24,16},{1,9},{9,1},{17,25},{25,17},{2,10},{10... | collective-permute-start | bytes 294920 | tf_op jit(solution)/shard_map/ppermute | solution.py:340
  98.9 1.3 collective-permute-start.21
  100.9 6.5 %inner.12 = (f32[3072,128]{1,0:T(8,128)S(1)}, f32[8,128]{1,0:T(8,128)S(1)}) custom-call(s32[8,4]{1,0:T(8,128)S(1)} %copy.40.columns, bf16[8,4,384,384]{3,2,1,0:T(8,128)(2,1)} %bitcast.84, bf16[8,384,128]{2,1,0:T(8,128)(2,1)S(1)} %copy-done.3), custom_call_target="tpu_custom_call" | custom-call | flops 1207959552 | bytes 12000000 | tf_op jit(solution)/shard_map/inner/pallas_call | solution.py:264
  108.0 1.6 %all-to-all-done.5 = bf16[32,48,128]{2,1,0:T(8,128)(2,1)S(1)} async-done(((bf16[32,48,128]{2,1,0:T(8,128)(2,1)}), bf16[32,48,128]{2,1,0:T(8,128)(2,1)S(1)}, u32[]{:S(2)}, u32[]{:S(2)}) %all-to-all-start.5) | async-done | bytes 393248 | tf_op jit(solution)/shard_map/all_to_all | solution.py:367
  109.6 4.0 %collective-permute-start.24 = (bf16[4,8,48,128]{3,2,1,0:T(8,128)(2,1)S(1)}, bf16[4,8,48,128]{3,2,1,0:T(8,128)(2,1)S(1)}, u32[]{:S(2)}, u32[]{:S(2)}) collective-permute-start(bf16[4,8,48,128]{3,2,1,0:T(8,128)(2,1)S(1)} %after.6.refs_2_), channel_id=1, source_target_pairs={{32,0},{33,1},{34,2},{35,3},{36,4},{37,5},{38,6},{39,7},{40,8},{41... | collective-permute-start | bytes 1179656 | tf_op jit(solution)/shard_map/ppermute | solution.py:435
  113.7 5.0 %outer.6.refs_1_ = f32[3072,128]{1,0:T(8,128)S(1)} custom-call(s32[8,4]{1,0:T(8,128)S(1)} %copy.40.columns, s32[3]{0:T(128)S(1)} %pad_add_fusion.refs_0_.flags, bf16[8,4,384,384]{3,2,1,0:T(8,128)(2,1)} %bitcast.85, f32[3072,128]{1,0:T(8,128)S(1)} %get-tuple-element.615.base, bf16[384,128]{1,0:T(8,128)(2,1)S(1)} %collective-permute-done.19.x_even.refs_1_, ...), custom_call_target="tpu_custom_call" | custom-call | flops 301989888 | bytes 6000000 | tf_op jit(solution)/shard_map/outer/pallas_call | solution.py:312
  118.7 2.3 %update.16 = (f32[3072,128]{1,0:T(8,128)}, f32[1,128]{1,0:T(1,128)S(1)}) custom-call(s32[3]{0:T(128)S(1)} %pad_add_fusion.refs_0_.flags, f32[3072,128]{1,0:T(8,128)S(1)} %outer.6.refs_1_, bf16[4,8,48,128]{3,2,1,0:T(8,128)(2,1)S(1)} %after.6.refs_2_, bf16[4,8,48,128]{3,2,1,0:T(8,128)(2,1)S(1)} %collective-permute-done.24.refs_3_, ...), custom_call_target="tpu_custom_call" | custom-call | tf_op jit(solution)/shard_map/update/pallas_call | solution.py:234
  121.1 11.7 %all_to_all.65 = f32[16,1,384]{2,1,0:T(1,128)S(1)} all-to-all(f32[16,1,384]{2,1,0:T(1,128)S(1)} %broadcast_in_dim.117), channel_id=1, replica_groups=mesh['zh'=4,'core'=2,'gx'=4,'y'=4,'zl'=2] {'gx','y'}, dimensions={0} | all-to-all | bytes 49152 | tf_op jit(solution)/shard_map/all_to_all | solution.py:351
  133.4 6.6 %all-to-all-start.7 = ((f32[16,1,384]{2,1,0:T(1,128)}), f32[16,1,384]{2,1,0:T(1,128)S(1)}, u32[]{:S(2)}, u32[]{:S(2)}) async-start(f32[16,1,384]{2,1,0:T(1,128)} %broadcast_in_dim.118), calls=%async_computation.7 | async-start | bytes 49152 | tf_op jit(solution)/shard_map/all_to_all | solution.py:351
  140.1 7.4 %all-to-all-done.7 = f32[16,1,384]{2,1,0:T(1,128)S(1)} async-done(((f32[16,1,384]{2,1,0:T(1,128)}), f32[16,1,384]{2,1,0:T(1,128)S(1)}, u32[]{:S(2)}, u32[]{:S(2)}) %all-to-all-start.7) | async-done | bytes 24608 | tf_op jit(solution)/shard_map/all_to_all | solution.py:351
  148.8 1.6 %conditional.1 = (f32[3,128]{1,0:T(4,128)S(1)}, f32[1,1,1,8,384,128]{5,4,3,2,1,0:T(8,128)S(1)}) conditional(s32[]{:T(128)} %convert_element_type.16, (s32[3]{0:T(128)S(1)}, f32[3072,128]{1,0:T(8,128)S(1)}, bf16[448,512]{1,0:T(8,128)(2,1)S(1)}, s32[]{:T(128)}, s32[8,4]{0,1:T(4,128)S(1)}, /*index=5*/bf16[8,4,384,384]{3,2,1,0:T(8,128)(2,1)}, ...), branch_computations={%region_3.9_spmd, %region_9.10_spmd} | conditional | flops 1510543616 | bytes 32378718 | solution.py:476
  148.9 1.5 %broadcast_multiply_fusion = f32[3072,128]{1,0:T(8,128)S(1)} fusion(f32[3072,128]{1,0:T(8,128)} %get-tuple-element.546, f32[128]{0:T(128)S(1)} %get-tuple-element.705), kind=kLoop, calls=%fused_computation.7 | loop fusion | flops 393216 | bytes 3146240 | tf_op jit(solution)/shard_map/cond/branch_1_fun/mul | solution.py:460
  (120 shorter events, 20.4 us)
Async XLA Ops:
  0.6 11.0 %copy-start.26 = (f32[1,8,7,1,8]{4,3,2,1,0:T(1,128)S(1)}, f32[1,8,7,1,8]{4,3,2,1,0:T(1,128)}, u32[]{:S(2)}) copy-start(f32[1,8,7,1,8]{4,3,2,1,0:T(1,128)} %param.17) | copy-start | bytes 5380
  6.0 18.1 %copy-start.29 = (s32[1,1,1,8,4]{3,4,2,1,0:T(4,128)S(1)}, s32[1,1,1,8,4]{3,4,2,1,0:T(4,128)}, u32[]{:S(2)}) copy-start(s32[1,1,1,8,4]{3,4,2,1,0:T(4,128)} %param.14) | copy-start | bytes 388
  6.1 18.2 %copy-start.1 = (bf16[8,384,128]{2,1,0:T(8,128)(2,1)S(1)}, bf16[8,384,128]{2,1,0:T(8,128)(2,1)}, u32[]{:S(2)}) copy-start(bf16[8,384,128]{2,1,0:T(8,128)(2,1)} %get-tuple-element.589.rounded) | copy-start | bytes 2359300
  6.1 6.9 %collective-permute-start.10 = (bf16[4,8,48,128]{3,2,1,0:T(8,128)(2,1)S(1)}, bf16[4,8,48,128]{3,2,1,0:T(8,128)(2,1)S(1)}, u32[]{:S(2)}, u32[]{:S(2)}) collective-permute-start(bf16[4,8,48,128]{3,2,1,0:T(8,128)(2,1)S(1)} %get-tuple-element.595), channel_id=1, source_target_pairs={{0,32},{32,0},{1,33},{33,1},{2,34},{34,2},{3,35},{35,3},{4,36},{36... | collective-permute-start | bytes 1179656 | tf_op jit(solution)/shard_map/ppermute | solution.py:430
  13.8 19.4 %all-to-all-start.3 = ((bf16[32,48,128]{2,1,0:T(8,128)(2,1)}), bf16[32,48,128]{2,1,0:T(8,128)(2,1)S(1)}, u32[]{:S(2)}, u32[]{:S(2)}) async-start(bf16[32,48,128]{2,1,0:T(8,128)(2,1)} %bitcast.22), calls=%async_computation.3 | async-start | bytes 786432 | tf_op jit(solution)/shard_map/all_to_all | solution.py:367
  20.2 10.6 %collective-permute-start.6 = (bf16[384,128]{1,0:T(8,128)(2,1)}, bf16[384,128]{1,0:T(8,128)(2,1)S(1)}, u32[]{:S(2)}, u32[]{:S(2)}) collective-permute-start(bf16[384,128]{1,0:T(8,128)(2,1)} %get-tuple-element.591), channel_id=1, source_target_pairs={{0,8},{8,0},{16,24},{24,16},{1,9},{9,1},{17,25},{25,17},{2,10},{10... | collective-permute-start | bytes 294920 | tf_op jit(solution)/shard_map/ppermute | solution.py:340
  21.5 9.3 %collective-permute-start.7 = (bf16[384,128]{1,0:T(8,128)(2,1)}, bf16[384,128]{1,0:T(8,128)(2,1)S(1)}, u32[]{:S(2)}, u32[]{:S(2)}) collective-permute-start(bf16[384,128]{1,0:T(8,128)(2,1)} %get-tuple-element.592), channel_id=1, source_target_pairs={{8,16},{16,8},{9,17},{17,9},{10,18},{18,10},{11,19},{19,11},{12,20... | collective-permute-start | bytes 294920 | tf_op jit(solution)/shard_map/ppermute | solution.py:341
  22.2 9.8 %collective-permute-start.8 = (bf16[384,128]{1,0:T(8,128)(2,1)}, bf16[384,128]{1,0:T(8,128)(2,1)S(1)}, u32[]{:S(2)}, u32[]{:S(2)}) collective-permute-start(bf16[384,128]{1,0:T(8,128)(2,1)} %get-tuple-element.593), channel_id=1, source_target_pairs={{0,1},{1,0},{2,3},{3,2},{4,5},{5,4},{6,7},{7,6},{8,9},{9,8},{10,11... | collective-permute-start | bytes 294920 | tf_op jit(solution)/shard_map/ppermute | solution.py:342
  23.5 8.5 %collective-permute-start.9 = (bf16[384,128]{1,0:T(8,128)(2,1)}, bf16[384,128]{1,0:T(8,128)(2,1)S(1)}, u32[]{:S(2)}, u32[]{:S(2)}) collective-permute-start(bf16[384,128]{1,0:T(8,128)(2,1)} %get-tuple-element.594), channel_id=1, source_target_pairs={{1,2},{2,1},{3,4},{4,3},{5,6},{6,5},{9,10},{10,9},{11,12},{12,11},... | collective-permute-start | bytes 294920 | tf_op jit(solution)/shard_map/ppermute | solution.py:343
  34.1 12.6 %collective-permute-start.11 = (bf16[4,8,48,128]{3,2,1,0:T(8,128)(2,1)S(1)}, bf16[4,8,48,128]{3,2,1,0:T(8,128)(2,1)}, u32[]{:S(2)}, u32[]{:S(2)}) collective-permute-start(bf16[4,8,48,128]{3,2,1,0:T(8,128)(2,1)S(1)} %after.4.refs_2_), channel_id=1, source_target_pairs={{32,0},{33,1},{34,2},{35,3},{36,4},{37,5},{38,6},{39,7},{40,8},{41... | collective-permute-start | bytes 1179656 | tf_op jit(solution)/shard_map/ppermute | solution.py:435
  40.0 6.7 %collective-permute-start.12 = (bf16[8,48,128]{2,1,0:T(8,128)(2,1)S(1)}, bf16[8,48,128]{2,1,0:T(8,128)(2,1)S(1)}, u32[]{:S(2)}, u32[]{:S(2)}) collective-permute-start(bf16[8,48,128]{2,1,0:T(8,128)(2,1)S(1)} %slice_bitcast_fusion), channel_id=1, source_target_pairs={{64,0},{65,1},{66,2},{67,3},{68,4},{69,5},{70,6},{71,7},{72,8},{73... | collective-permute-start | bytes 294920 | tf_op jit(solution)/shard_map/ppermute | solution.py:441
  41.7 5.1 %copy-start.7 = (bf16[4,8,48,128]{3,2,1,0:T(8,128)(2,1)S(1)}, bf16[4,8,48,128]{3,2,1,0:T(8,128)(2,1)}, u32[]{:S(2)}) copy-start(bf16[4,8,48,128]{3,2,1,0:T(8,128)(2,1)} %get-tuple-element.599.refs_5_) | copy-start | bytes 1179652
  50.6 15.0 %copy-start.2 = (bf16[8,384,128]{2,1,0:T(8,128)(2,1)S(1)}, bf16[8,384,128]{2,1,0:T(8,128)(2,1)}, u32[]{:S(2)}) copy-start(bf16[8,384,128]{2,1,0:T(8,128)(2,1)} %get-tuple-element.601.rounded) | copy-start | bytes 2359300
  50.6 3.7 %collective-permute-start.17 = (bf16[4,8,48,128]{3,2,1,0:T(8,128)(2,1)S(1)}, bf16[4,8,48,128]{3,2,1,0:T(8,128)(2,1)S(1)}, u32[]{:S(2)}, u32[]{:S(2)}) collective-permute-start(bf16[4,8,48,128]{3,2,1,0:T(8,128)(2,1)S(1)} %get-tuple-element.607), channel_id=1, source_target_pairs={{0,32},{32,0},{1,33},{33,1},{2,34},{34,2},{3,35},{35,3},{4,36},{36... | collective-permute-start | bytes 1179656 | tf_op jit(solution)/shard_map/ppermute | solution.py:430
  55.3 18.0 %all-to-all-start.4 = ((bf16[32,48,128]{2,1,0:T(8,128)(2,1)}), bf16[32,48,128]{2,1,0:T(8,128)(2,1)S(1)}, u32[]{:S(2)}, u32[]{:S(2)}) async-start(bf16[32,48,128]{2,1,0:T(8,128)(2,1)} %bitcast.25), calls=%async_computation.4 | async-start | bytes 786432 | tf_op jit(solution)/shard_map/all_to_all | solution.py:367
  60.1 12.0 %collective-permute-start.13 = (bf16[384,128]{1,0:T(8,128)(2,1)}, bf16[384,128]{1,0:T(8,128)(2,1)S(1)}, u32[]{:S(2)}, u32[]{:S(2)}) collective-permute-start(bf16[384,128]{1,0:T(8,128)(2,1)} %get-tuple-element.603), channel_id=1, source_target_pairs={{0,8},{8,0},{16,24},{24,16},{1,9},{9,1},{17,25},{25,17},{2,10},{10... | collective-permute-start | bytes 294920 | tf_op jit(solution)/shard_map/ppermute | solution.py:340
  62.9 9.2 %collective-permute-start.14 = (bf16[384,128]{1,0:T(8,128)(2,1)}, bf16[384,128]{1,0:T(8,128)(2,1)S(1)}, u32[]{:S(2)}, u32[]{:S(2)}) collective-permute-start(bf16[384,128]{1,0:T(8,128)(2,1)} %get-tuple-element.604), channel_id=1, source_target_pairs={{8,16},{16,8},{9,17},{17,9},{10,18},{18,10},{11,19},{19,11},{12,20... | collective-permute-start | bytes 294920 | tf_op jit(solution)/shard_map/ppermute | solution.py:341
  63.6 8.6 %collective-permute-start.15 = (bf16[384,128]{1,0:T(8,128)(2,1)S(1)}, bf16[384,128]{1,0:T(8,128)(2,1)S(1)}, u32[]{:S(2)}, u32[]{:S(2)}) collective-permute-start(bf16[384,128]{1,0:T(8,128)(2,1)S(1)} %get-tuple-element.605), channel_id=1, source_target_pairs={{0,1},{1,0},{2,3},{3,2},{4,5},{5,4},{6,7},{7,6},{8,9},{9,8},{10,11... | collective-permute-start | bytes 294920 | tf_op jit(solution)/shard_map/ppermute | solution.py:342
  64.9 7.3 %collective-permute-start.16 = (bf16[384,128]{1,0:T(8,128)(2,1)S(1)}, bf16[384,128]{1,0:T(8,128)(2,1)S(1)}, u32[]{:S(2)}, u32[]{:S(2)}) collective-permute-start(bf16[384,128]{1,0:T(8,128)(2,1)S(1)} %get-tuple-element.606), channel_id=1, source_target_pairs={{1,2},{2,1},{3,4},{4,3},{5,6},{6,5},{9,10},{10,9},{11,12},{12,11},... | collective-permute-start | bytes 294920 | tf_op jit(solution)/shard_map/ppermute | solution.py:343
  73.2 9.9 %collective-permute-start.18 = (bf16[4,8,48,128]{3,2,1,0:T(8,128)(2,1)S(1)}, bf16[4,8,48,128]{3,2,1,0:T(8,128)(2,1)S(1)}, u32[]{:S(2)}, u32[]{:S(2)}) collective-permute-start(bf16[4,8,48,128]{3,2,1,0:T(8,128)(2,1)S(1)} %after.5.refs_2_), channel_id=1, source_target_pairs={{32,0},{33,1},{34,2},{35,3},{36,4},{37,5},{38,6},{39,7},{40,8},{41... | collective-permute-start | bytes 1179656 | tf_op jit(solution)/shard_map/ppermute | solution.py:435
  86.5 14.4 %copy-start.3 = (bf16[8,384,128]{2,1,0:T(8,128)(2,1)S(1)}, bf16[8,384,128]{2,1,0:T(8,128)(2,1)}, u32[]{:S(2)}) copy-start(bf16[8,384,128]{2,1,0:T(8,128)(2,1)} %get-tuple-element.614.rounded) | copy-start | bytes 2359300
  86.5 3.7 %collective-permute-start.23 = (bf16[4,8,48,128]{3,2,1,0:T(8,128)(2,1)S(1)}, bf16[4,8,48,128]{3,2,1,0:T(8,128)(2,1)S(1)}, u32[]{:S(2)}, u32[]{:S(2)}) collective-permute-start(bf16[4,8,48,128]{3,2,1,0:T(8,128)(2,1)S(1)} %get-tuple-element.620), channel_id=1, source_target_pairs={{0,32},{32,0},{1,33},{33,1},{2,34},{34,2},{3,35},{35,3},{4,36},{36... | collective-permute-start | bytes 1179656 | tf_op jit(solution)/shard_map/ppermute | solution.py:430
  91.1 18.5 %all-to-all-start.5 = ((bf16[32,48,128]{2,1,0:T(8,128)(2,1)}), bf16[32,48,128]{2,1,0:T(8,128)(2,1)S(1)}, u32[]{:S(2)}, u32[]{:S(2)}) async-start(bf16[32,48,128]{2,1,0:T(8,128)(2,1)} %bitcast.27), calls=%async_computation.5 | async-start | bytes 786432 | tf_op jit(solution)/shard_map/all_to_all | solution.py:367
  95.9 11.5 %collective-permute-start.19 = (bf16[384,128]{1,0:T(8,128)(2,1)}, bf16[384,128]{1,0:T(8,128)(2,1)S(1)}, u32[]{:S(2)}, u32[]{:S(2)}) collective-permute-start(bf16[384,128]{1,0:T(8,128)(2,1)} %get-tuple-element.616), channel_id=1, source_target_pairs={{0,8},{8,0},{16,24},{24,16},{1,9},{9,1},{17,25},{25,17},{2,10},{10... | collective-permute-start | bytes 294920 | tf_op jit(solution)/shard_map/ppermute | solution.py:340
  98.2 9.2 %collective-permute-start.20 = (bf16[384,128]{1,0:T(8,128)(2,1)}, bf16[384,128]{1,0:T(8,128)(2,1)S(1)}, u32[]{:S(2)}, u32[]{:S(2)}) collective-permute-start(bf16[384,128]{1,0:T(8,128)(2,1)} %get-tuple-element.617), channel_id=1, source_target_pairs={{8,16},{16,8},{9,17},{17,9},{10,18},{18,10},{11,19},{19,11},{12,20... | collective-permute-start | bytes 294920 | tf_op jit(solution)/shard_map/ppermute | solution.py:341
  98.9 9.1 %collective-permute-start.21 = (bf16[384,128]{1,0:T(8,128)(2,1)S(1)}, bf16[384,128]{1,0:T(8,128)(2,1)S(1)}, u32[]{:S(2)}, u32[]{:S(2)}) collective-permute-start(bf16[384,128]{1,0:T(8,128)(2,1)S(1)} %get-tuple-element.618), channel_id=1, source_target_pairs={{0,1},{1,0},{2,3},{3,2},{4,5},{5,4},{6,7},{7,6},{8,9},{9,8},{10,11... | collective-permute-start | bytes 294920 | tf_op jit(solution)/shard_map/ppermute | solution.py:342
  100.2 7.8 %collective-permute-start.22 = (bf16[384,128]{1,0:T(8,128)(2,1)S(1)}, bf16[384,128]{1,0:T(8,128)(2,1)S(1)}, u32[]{:S(2)}, u32[]{:S(2)}) collective-permute-start(bf16[384,128]{1,0:T(8,128)(2,1)S(1)} %get-tuple-element.619), channel_id=1, source_target_pairs={{1,2},{2,1},{3,4},{4,3},{5,6},{6,5},{9,10},{10,9},{11,12},{12,11},... | collective-permute-start | bytes 294920 | tf_op jit(solution)/shard_map/ppermute | solution.py:343
  109.6 9.0 %collective-permute-start.24 = (bf16[4,8,48,128]{3,2,1,0:T(8,128)(2,1)S(1)}, bf16[4,8,48,128]{3,2,1,0:T(8,128)(2,1)S(1)}, u32[]{:S(2)}, u32[]{:S(2)}) collective-permute-start(bf16[4,8,48,128]{3,2,1,0:T(8,128)(2,1)S(1)} %after.6.refs_2_), channel_id=1, source_target_pairs={{32,0},{33,1},{34,2},{35,3},{36,4},{37,5},{38,6},{39,7},{40,8},{41... | collective-permute-start | bytes 1179656 | tf_op jit(solution)/shard_map/ppermute | solution.py:435
  118.7 30.1 %copy-start.15 = (bf16[448,512]{1,0:T(8,128)(2,1)S(1)}, bf16[448,512]{1,0:T(8,128)(2,1)}, u32[]{:S(2)}) copy-start(bf16[448,512]{1,0:T(8,128)(2,1)} %copy-done.12) | copy-start | bytes 1376260
  118.7 30.1 %copy-start.19 = (bf16[512,448]{1,0:T(8,128)(2,1)S(1)}, bf16[512,448]{1,0:T(8,128)(2,1)}, u32[]{:S(2)}) copy-start(bf16[512,448]{1,0:T(8,128)(2,1)} %fusion.refs_7_) | copy-start | bytes 1376260
  118.7 30.1 %copy-start.24 = (f32[1,1,1,8,384,128]{5,4,3,2,1,0:T(8,128)S(1)}, f32[1,1,1,8,384,128]{5,4,3,2,1,0:T(8,128)}, u32[]{:S(2)}) copy-start(f32[1,1,1,8,384,128]{5,4,3,2,1,0:T(8,128)} %param.12) | copy-start | bytes 4718596
  133.4 14.0 %all-to-all-start.7 = ((f32[16,1,384]{2,1,0:T(1,128)}), f32[16,1,384]{2,1,0:T(1,128)S(1)}, u32[]{:S(2)}, u32[]{:S(2)}) async-start(f32[16,1,384]{2,1,0:T(1,128)} %broadcast_in_dim.118), calls=%async_computation.7 | async-start | bytes 49152 | tf_op jit(solution)/shard_map/all_to_all | solution.py:351
  (18 other events, 66.1 us)
where the time goes:
time: 153 us; the launch traced here: 152 us
  starting transfers between devices  62 us (41%)
  Pallas kernels  47.4 us (31%)
  waiting for transfers between devices  16.6 us (11%)
  blocking collectives  11.7 us (8%)
  other arithmetic  6.15 us (4%)
  local copies, waits for them, and re-layouts  5.63 us (4%)
  between operations  2.09 us (1%)
    pallas_call x3, Pallas kernels, inner(): pl.pallas_call(inner_kernel, out_shape=[jax.ShapeDtypeStruct((ROWS, S), F...  19.6 us
    all_to_all x3, starting transfers between devices, exchange(): lax.all_to_all(send.reshape(PAIRS * GY_N, MESSAGE, S), ('zh', 'y', 'zl'),...  16 us
    pallas_call x3, Pallas kernels, outer(): pl.pallas_call(outer_kernel, out_shape=jax.ShapeDtypeStruct((ROWS, S), F3...  14.9 us
    ppermute x3, starting transfers between devices, step(): handed = lax.ppermute(received, GROUP, [(1, 0)])  14.8 us
    pallas_call x4, Pallas kernels, update(): pl.pallas_call(functools.partial(update_kernel, turn, scaled), out_shape=...  12.8 us
    all_to_all x1, blocking collectives, total_of(): lax.all_to_all(spread, axes, split_axis=0, concat_axis=0, tiled=True)  11.7 us
    ppermute x3, starting transfers between devices, step(): passed = lax.ppermute(send_b, GROUP, [(0, 1), (1, 0)])  9.64 us
    all_to_all x1, waiting for transfers between devices, total_of(): lax.all_to_all(spread, axes, split_axis=0, concat_axis=0, tiled=True)  7.36 us
  transfers between devices with their start and end apart: 23, of which 9 were waited for; matrix products, arithmetic and copies ran while one was open for 1% of the time, Pallas kernels for 23%

commit v1 on v0

--- a/solution.py
+++ b/solution.py
@@ -11,6 +11,7 @@
 TILE = 384
 NB = 8
 KB = 4
+NEAR = NB + 2
 S = 128
 CAP = 8
 DOFS = 6
@@ -116,7 +117,7 @@
         def _():
             if turn == 1:
                 kappa[...] = kappa_in[...]
-            difference(0, own_a.at[0], received.at[0])
+            difference(0, own_b.at[0], received.at[0])
             slots[GY_N : 2 * GY_N] = jnp.zeros((GY_N, DOFS, CAP, S), F32)
 
         def pair_of(count, d):
@@ -132,25 +133,28 @@
             y[pl.ds(d, NODES, stride=DOFS), :] = value
             return jnp.sum(jnp.square(value).reshape(NODES // 8, 8, S), axis=0)
 
+        def couple(coupling_of):
+            total = jnp.zeros((8, S), F32)
+            for d in range(0, DOFS, 2):
+                coupling = coupling_of(d)
+                total += finish(d, coupling[:, :S]) + finish(d + 1, coupling[:, S:])
+            squares[...] = jnp.sum(total, axis=0, keepdims=True)
+
         @on_rod
         def _():
-            total = jnp.zeros((8, S), F32)
-            for d in range(0, DOFS, 2):
-                coupling = dot(scatter[...], pair_of(MEMB * GY_N, d).astype(BF16))
-                total += finish(d, coupling[:, :S]) + finish(d + 1, coupling[:, S:])
-            squares[...] = jnp.sum(total, axis=0, keepdims=True)
+            couple(lambda d: dot(scatter[...], pair_of(MEMB * GY_N, d).astype(BF16)))
 
         @on_membrane
         def _():
-            total = jnp.zeros((8, S), F32)
             place = scatter[:, : 2 * MSLOTS]
-            for d in range(0, DOFS, 2):
+
+            def coupling_of(d):
                 delta = pair_of(2 * GY_N, d)
                 high = delta.astype(BF16)
                 low = (delta - high.astype(F32)).astype(BF16)
-                coupling = dot(place, high) + dot(place, low)
-                total += finish(d, coupling[:, :S]) + finish(d + 1, coupling[:, S:])
-            squares[...] = jnp.sum(total, axis=0, keepdims=True)
+                return dot(place, high) + dot(place, low)
+
+            couple(coupling_of)
 
     if not last:
         source = base if first else y
@@ -165,38 +169,39 @@
         y_even[...] = rounded[1 + (NB - 3) * odd_y]
         y_odd[...] = rounded[NB - 2 - (NB - 3) * odd_y]
 
-        def collect(count):
+        def collect(count, put):
             pick = gather[: count * MSLOTS]
             for d in range(0, DOFS, 2):
                 values = jnp.concatenate(
                     [source[pl.ds(d + e, NODES, stride=DOFS), :].astype(BF16) for e in range(2)],
                     axis=1,
                 )
-                rows = dot(pick, values)
-                for e in range(2):
-                    slots[: count * GY_N, d + e] = rows[:, e * S : (e + 1) * S].reshape(
-                        count * GY_N, CAP, S
-                    )
-
-        def message(q):
-            return slots[q * GY_N : (q + 1) * GY_N].reshape(GY_N, MESSAGE, S).astype(BF16)
+                found = dot(pick, values)
+                both = [
+                    found[:, e * S : (e + 1) * S].reshape(count * GY_N, 1, CAP, S) for e in range(2)
+                ]
+                rows = jnp.concatenate(both, axis=1).reshape(count * GY_N, 2 * CAP, S).astype(BF16)
+                for q in range(count):
+                    put(q, d, rows[q * GY_N : (q + 1) * GY_N])
 
         nothing = jnp.zeros((GY_N, MESSAGE, S), BF16)
 
         @on_rod
         def _():
-            collect(MEMB)
+            def put(q, d, rows):
+                target = send_a if q % 2 else send_b
+                target[(q + 1) // 2, :, d * CAP : (d + 2) * CAP] = rows
+
+            collect(MEMB, put)
             send_a[0] = nothing
-            send_b[0] = message(0)
-            for q in range(1, PAIRS):
-                send_a[q] = message(2 * q - 1)
-                send_b[q] = message(2 * q)
 
         @on_membrane
         def _():
-            collect(1)
-            send_a[0] = message(0)
-            send_b[0] = message(0)
+            def put(q, d, rows):
+                send_a[0, :, d * CAP : (d + 2) * CAP] = rows
+                send_b[0, :, d * CAP : (d + 2) * CAP] = rows
+
+            collect(1, put)
             for q in range(1, PAIRS):
                 send_a[q] = nothing
                 send_b[q] = nothing
@@ -242,89 +247,102 @@
     )(*args)
 
 
-def inner_kernel(columns, blocks, rounded, out, token, extended, copied):
-    copy = pltpu.make_async_copy(rounded, extended.at[:NB], copied)
-    copy.start()
-    extended[NB] = jnp.zeros((TILE, S), BF16)
-    copy.wait()
+def inner_kernel(columns, flags, blocks, rounded, x_even, x_odd, *refs):
+    (out, token, extended, tiles, copied) = refs
+    half = NB // 2
+    copies = [pltpu.make_async_copy(rounded, extended.at[:NB], copied.at[2])]
+    for part in range(2):
+        rows = pl.ds(part * half, half)
+        copies.append(pltpu.make_async_copy(blocks.at[rows], tiles.at[rows], copied.at[part]))
+    for copy in copies:
+        copy.start()
+    odd_x = flags[1]
+    extended[NB + 1 - odd_x] = x_even[...]
+    extended[NB + odd_x] = x_odd[...]
+    extended[NEAR] = jnp.zeros((TILE, S), BF16)
+    copies[0].wait()
 
     def row_of(r, _):
-        row = jnp.concatenate([blocks[r, k] for k in range(KB)], axis=1)
+        row = jnp.concatenate([tiles[r, k] for k in range(KB)], axis=1)
         picked = jnp.concatenate(
-            [extended[jnp.minimum(columns[r, k], NB)] for k in range(KB)], axis=0
+            [extended[jnp.minimum(columns[r, k], NEAR)] for k in range(KB)], axis=0
         )
         out[pl.ds(pl.multiple_of(r * TILE, TILE), TILE)] = dot(row, picked)
         return 0
 
-    lax.fori_loop(0, NB, row_of, 0, unroll=4)
+    for part in range(2):
+        copies[part + 1].wait()
+        lax.fori_loop(part * half, (part + 1) * half, row_of, 0, unroll=2)
     token[...] = out[:8]
 
 
-def inner(columns, blocks, rounded):
+def inner(columns, flags, blocks, rounded, x_even, x_odd):
     return pl.pallas_call(
         inner_kernel,
         out_shape=[jax.ShapeDtypeStruct((ROWS, S), F32), jax.ShapeDtypeStruct((8, S), F32)],
-        in_specs=[SMEM, VMEM, HBM],
+        in_specs=[SMEM, SMEM, HBM, HBM, VMEM, VMEM],
         out_specs=[VMEM, VMEM],
-        scratch_shapes=[pltpu.VMEM((NB + 1, TILE, S), BF16), pltpu.SemaphoreType.DMA],
+        scratch_shapes=[
+            pltpu.VMEM((NEAR + 1, TILE, S), BF16),
+            pltpu.VMEM((NB, KB, TILE, TILE), BF16),
+            pltpu.SemaphoreType.DMA((3,)),
+        ],
         compiler_params=pltpu.CompilerParams(vmem_limit_bytes=VMEM_BYTES),
         cost_estimate=pl.CostEstimate(
             flops=2 * NB * KB * TILE * TILE * S, bytes_accessed=12_000_000, transcendentals=0
         ),
         name="inner",
-    )(columns, blocks, rounded)
-
-
-def outer_kernel(columns, flags, blocks, base, x_even, x_odd, y_even, y_odd, out, edges, tiles, copied):
+    )(columns, flags, blocks, rounded, x_even, x_odd)
+
+
+def outer_kernel(columns, flags, blocks, base, y_even, y_odd, out, edges, tiles, copied):
     def copy_of(r, k):
         j = r * (KB - 1) + k - 1
         return pltpu.make_async_copy(blocks.at[r, k], tiles.at[j], copied.at[j])
 
     def fetch(r, _):
         for k in range(1, KB):
-            pl.when(columns[r, k] >= NB)(copy_of(r, k).start)
+            pl.when(columns[r, k] >= NEAR)(copy_of(r, k).start)
         return 0
 
     lax.fori_loop(0, NB, fetch, 0)
-    odd_x, odd_y = flags[1], flags[2]
-    edges[1 - odd_x] = x_even[...]
-    edges[odd_x] = x_odd[...]
-    edges[3 - odd_y] = y_even[...]
-    edges[2 + odd_y] = y_odd[...]
+    odd_y = flags[2]
+    edges[1 - odd_y] = y_even[...]
+    edges[odd_y] = y_odd[...]
 
     def add(r, _):
         rows = pl.ds(pl.multiple_of(r * TILE, TILE), TILE)
         out[rows] = base[rows]
         for k in range(1, KB):
 
-            @pl.when(columns[r, k] >= NB)
+            @pl.when(columns[r, k] >= NEAR)
             def _():
                 copy_of(r, k).wait()
-                out[rows] += dot(tiles[r * (KB - 1) + k - 1], edges[columns[r, k] - NB])
+                out[rows] += dot(tiles[r * (KB - 1) + k - 1], edges[columns[r, k] - NEAR])
 
         return 0
 
     lax.fori_loop(0, NB, add, 0)
 
 
-def outer(columns, flags, blocks, base, halo):
+def outer(columns, flags, blocks, base, y_even, y_odd):
     count = NB * (KB - 1)
     return pl.pallas_call(
         outer_kernel,
         out_shape=jax.ShapeDtypeStruct((ROWS, S), F32),
-        in_specs=[SMEM, SMEM, HBM] + [VMEM] * 5,
+        in_specs=[SMEM, SMEM, HBM] + [VMEM] * 3,
         out_specs=VMEM,
         scratch_shapes=[
-            pltpu.VMEM((4, TILE, S), BF16),
+            pltpu.VMEM((2, TILE, S), BF16),
             pltpu.VMEM((count, TILE, TILE), BF16),
             pltpu.SemaphoreType.DMA((count,)),
         ],
         compiler_params=pltpu.CompilerParams(vmem_limit_bytes=VMEM_BYTES),
         cost_estimate=pl.CostEstimate(
-            flops=8 * 2 * TILE * TILE * S, bytes_accessed=6_000_000, transcendentals=0
+            flops=4 * 2 * TILE * TILE * S, bytes_accessed=6_000_000, transcendentals=0
         ),
         name="outer",
-    )(columns, flags, blocks, base, *halo)
+    )(columns, flags, blocks, base, y_even, y_odd)
 
 
 def swaps(count, start):
@@ -429,11 +447,11 @@
         (rounded, *edges, send_a, send_b, own_a, own_b) = state[:9]
         passed = lax.ppermute(send_b, GROUP, [(0, 1), (1, 0)])
         received = exchange(merge(group, send_a, passed, stiff_message if turn == 1 else None))
-        halo = halos(edges)
-        (part, token) = inner(columns, blocks, rounded)
-        received = after(received, [token, *halo])
+        (x_even, x_odd, y_even, y_odd) = halos(edges)
+        (part, token) = inner(columns, flags, blocks, rounded, x_even, x_odd)
+        received = after(received, [token, y_even, y_odd])
         handed = lax.ppermute(received, GROUP, [(1, 0)])
-        base = outer(columns, flags, blocks, part, halo)
+        base = outer(columns, flags, blocks, part, y_even, y_odd)
         args = [flags, base, received, handed, own_a, own_b, kappa, scatter]
         if turn < MATVECS:
             args += [gather]

time: 153 us -> 147 us (0.961)
  Pallas kernels: 47.4 us -> 38.3 us
  waiting for transfers between devices: 16.6 us -> 18.6 us
  blocking collectives: 11.7 us -> 13.6 us
  starting transfers between devices: 62 us -> 63.7 us
  local copies, waits for them, and re-layouts: 5.63 us -> 4.09 us
    pallas_call x3, Pallas kernels: 14.9 us -> 8.35 us  [outer(): pl.pallas_call(outer_kernel, out_shape=jax.ShapeDtypeStruct((ROWS, S), F3...]
    ppermute x3, starting transfers between devices: 9.64 us -> 13.3 us  [step(): passed = lax.ppermute(send_b, GROUP, [(0, 1), (1, 0)])]
    all_to_all x1, blocking collectives: 11.7 us -> 13.6 us  [total_of(): lax.all_to_all(spread, axes, split_axis=0, concat_axis=0, tiled=True)]
    ppermute x3, waiting for transfers between devices: 1.71 us -> 3.27 us  [halos(): lax.ppermute(y_even, GY, swaps(GY_N, 0))]
    unnamed x55 -> x53, local copies, waits for them, and re-layouts: 3.62 us -> 2.08 us
  transfers between devices with their start and end apart: 23 -> 23, of which waited for: 9 -> 10; matrix products, arithmetic and copies ran while one was open for 1% -> 1% of each run, Pallas kernels for 23% -> 18%
where the time goes in v1:
time: 147 us
  starting transfers between devices  63.7 us (43%)
  Pallas kernels  38.3 us (26%)
  waiting for transfers between devices  18.6 us (13%)
  blocking collectives  13.6 us (9%)
  other arithmetic  6.13 us (4%)
  local copies, waits for them, and re-layouts  4.09 us (3%)
  between operations  2.1 us (1%)
    pallas_call x3, Pallas kernels, inner(): pl.pallas_call(inner_kernel, out_shape=[jax.ShapeDtypeStruct((ROWS, S), F...  18.4 us
    all_to_all x3, starting transfers between devices, exchange(): lax.all_to_all(send.reshape(PAIRS * GY_N, MESSAGE, S), ('zh', 'y', 'zl'),...  15.8 us
    ppermute x3, starting transfers between devices, step(): handed = lax.ppermute(received, GROUP, [(1, 0)])  14 us
    all_to_all x1, blocking collectives, total_of(): lax.all_to_all(spread, axes, split_axis=0, concat_axis=0, tiled=True)  13.6 us
    ppermute x3, starting transfers between devices, step(): passed = lax.ppermute(send_b, GROUP, [(0, 1), (1, 0)])  13.3 us
    pallas_call x4, Pallas kernels, update(): pl.pallas_call(functools.partial(update_kernel, turn, scaled), out_shape=...  11.4 us
    pallas_call x3, Pallas kernels, outer(): pl.pallas_call(outer_kernel, out_shape=jax.ShapeDtypeStruct((ROWS, S), F3...  8.35 us
    all_to_all x1, waiting for transfers between devices, total_of(): lax.all_to_all(spread, axes, split_axis=0, concat_axis=0, tiled=True)  7.36 us
  transfers between devices with their start and end apart: 23, of which 10 were waited for; matrix products, arithmetic and copies ran while one was open for 1% of the time, Pallas kernels for 18%

profile of v1, /device:TPU:1, one launch (start us, length us, event | category | flops | bytes accessed | tf_op | source)
XLA Modules:
  0.0 146.6 jit_solution(13102804420616848126)
XLA Ops:
  2.6 3.3 %update.13 = (bf16[8,384,128]{2,1,0:T(8,128)(2,1)}, bf16[384,128]{1,0:T(8,128)(2,1)S(1)}, bf16[384,128]{1,0:T(8,128)(2,1)S(1)}, bf16[384,128]{1,0:T(8,128)(2,1)}...) custom-call(s32[3]{0:T(128)S(1)} %pad_add_fusion.refs_0_.flags, ...), custom_call_target="tpu_custom_call" | custom-call | tf_op jit(solution)/shard_map/update/pallas_call | solution.py:239
  5.9 5.5 %collective-permute-start.10 = (bf16[4,8,48,128]{3,2,1,0:T(8,128)(2,1)S(1)}, bf16[4,8,48,128]{3,2,1,0:T(8,128)(2,1)S(1)}, u32[]{:S(2)}, u32[]{:S(2)}) collective-permute-start(bf16[4,8,48,128]{3,2,1,0:T(8,128)(2,1)S(1)} %get-tuple-element.595), channel_id=1, source_target_pairs={{0,32},{32,0},{1,33},{33,1},{2,34},{34,2},{3,35},{35,3},{4,36},{36... | collective-permute-start | bytes 1179656 | tf_op jit(solution)/shard_map/ppermute | solution.py:448
  13.6 6.4 %all-to-all-start.3 = ((bf16[32,48,128]{2,1,0:T(8,128)(2,1)}), bf16[32,48,128]{2,1,0:T(8,128)(2,1)S(1)}, u32[]{:S(2)}, u32[]{:S(2)}) async-start(bf16[32,48,128]{2,1,0:T(8,128)(2,1)} %bitcast.22), calls=%async_computation.3 | async-start | bytes 786432 | tf_op jit(solution)/shard_map/all_to_all | solution.py:385
  22.0 1.3 collective-permute-start.8
  24.1 6.1 %inner.10 = (f32[3072,128]{1,0:T(8,128)S(1)}, f32[8,128]{1,0:T(8,128)S(1)}) custom-call(s32[8,4]{1,0:T(8,128)S(1)} %copy.40.columns, s32[3]{0:T(128)S(1)} %pad_add_fusion.refs_0_.flags, bf16[8,4,384,384]{3,2,1,0:T(8,128)(2,1)} %bitcast.80, bf16[8,384,128]{2,1,0:T(8,128)(2,1)S(1)} %copy-done.1, bf16[384,128]{1,0:T(8,128)(2,1)S(1)} %collective-permute-done.6.x_even, ...), custom_call_target="tpu_custom_call" | custom-call | flops 1207959552 | bytes 12000000 | tf_op jit(solution)/shard_map/inner/pallas_call | solution.py:280
  30.3 1.6 %collective-permute-done.8.y_even.refs_1_ = bf16[384,128]{1,0:T(8,128)(2,1)S(1)} collective-permute-done((bf16[384,128]{1,0:T(8,128)(2,1)}, bf16[384,128]{1,0:T(8,128)(2,1)S(1)}, u32[]{:S(2)}, u32[]{:S(2)}) %collective-permute-start.8) | collective-permute-done | bytes 98336 | tf_op jit(solution)/shard_map/ppermute | solution.py:360
  33.1 5.1 %collective-permute-start.11 = (bf16[4,8,48,128]{3,2,1,0:T(8,128)(2,1)S(1)}, bf16[4,8,48,128]{3,2,1,0:T(8,128)(2,1)S(1)}, u32[]{:S(2)}, u32[]{:S(2)}) collective-permute-start(bf16[4,8,48,128]{3,2,1,0:T(8,128)(2,1)S(1)} %after.4.refs_2_), channel_id=1, source_target_pairs={{32,0},{33,1},{34,2},{35,3},{36,4},{37,5},{38,6},{39,7},{40,8},{41... | collective-permute-start | bytes 1179656 | tf_op jit(solution)/shard_map/ppermute | solution.py:453
  40.0 2.8 %outer.4.refs_1_ = f32[3072,128]{1,0:T(8,128)S(1)} custom-call(s32[8,4]{1,0:T(8,128)S(1)} %copy.40.columns, s32[3]{0:T(128)S(1)} %pad_add_fusion.refs_0_.flags, bf16[8,4,384,384]{3,2,1,0:T(8,128)(2,1)} %bitcast.81, f32[3072,128]{1,0:T(8,128)S(1)} %get-tuple-element.592.base, bf16[384,128]{1,0:T(8,128)(2,1)S(1)} %collective-permute-done.8.y_even.refs_1_, ...), custom_call_target="tpu_custom_call" | custom-call | flops 150994944 | bytes 6000000 | tf_op jit(solution)/shard_map/outer/pallas_call | solution.py:330
  42.9 3.2 %update.14 = (bf16[8,384,128]{2,1,0:T(8,128)(2,1)}, bf16[384,128]{1,0:T(8,128)(2,1)S(1)}, bf16[384,128]{1,0:T(8,128)(2,1)S(1)}, bf16[384,128]{1,0:T(8,128)(2,1)}...) custom-call(s32[3]{0:T(128)S(1)} %pad_add_fusion.refs_0_.flags, ...), custom_call_target="tpu_custom_call" | custom-call | tf_op jit(solution)/shard_map/update/pallas_call | solution.py:239
  46.2 5.7 %collective-permute-start.17 = (bf16[4,8,48,128]{3,2,1,0:T(8,128)(2,1)S(1)}, bf16[4,8,48,128]{3,2,1,0:T(8,128)(2,1)S(1)}, u32[]{:S(2)}, u32[]{:S(2)}) collective-permute-start(bf16[4,8,48,128]{3,2,1,0:T(8,128)(2,1)S(1)} %get-tuple-element.607), channel_id=1, source_target_pairs={{0,32},{32,0},{1,33},{33,1},{2,34},{34,2},{3,35},{35,3},{4,36},{36... | collective-permute-start | bytes 1179656 | tf_op jit(solution)/shard_map/ppermute | solution.py:448
  51.9 1.3 collective-permute-done.17
  54.1 4.3 %all-to-all-start.4 = ((bf16[32,48,128]{2,1,0:T(8,128)(2,1)}), bf16[32,48,128]{2,1,0:T(8,128)(2,1)S(1)}, u32[]{:S(2)}, u32[]{:S(2)}) async-start(bf16[32,48,128]{2,1,0:T(8,128)(2,1)} %bitcast.25), calls=%async_computation.4 | async-start | bytes 786432 | tf_op jit(solution)/shard_map/all_to_all | solution.py:385
  58.4 1.9 %collective-permute-start.13 = (bf16[384,128]{1,0:T(8,128)(2,1)S(1)}, bf16[384,128]{1,0:T(8,128)(2,1)S(1)}, u32[]{:S(2)}, u32[]{:S(2)}) collective-permute-start(bf16[384,128]{1,0:T(8,128)(2,1)S(1)} %get-tuple-element.602), channel_id=1, source_target_pairs={{0,8},{8,0},{16,24},{24,16},{1,9},{9,1},{17,25},{25,17},{2,10},{10... | collective-permute-start | bytes 294920 | tf_op jit(solution)/shard_map/ppermute | solution.py:358
  61.0 1.3 collective-permute-start.15
  63.0 6.1 %inner.11 = (f32[3072,128]{1,0:T(8,128)S(1)}, f32[8,128]{1,0:T(8,128)S(1)}) custom-call(s32[8,4]{1,0:T(8,128)S(1)} %copy.40.columns, s32[3]{0:T(128)S(1)} %pad_add_fusion.refs_0_.flags, bf16[8,4,384,384]{3,2,1,0:T(8,128)(2,1)} %bitcast.82, bf16[8,384,128]{2,1,0:T(8,128)(2,1)S(1)} %copy-done.2, bf16[384,128]{1,0:T(8,128)(2,1)S(1)} %collective-permute-done.13.x_even, ...), custom_call_target="tpu_custom_call" | custom-call | flops 1207959552 | bytes 12000000 | tf_op jit(solution)/shard_map/inner/pallas_call | solution.py:280
  71.6 4.9 %collective-permute-start.18 = (bf16[4,8,48,128]{3,2,1,0:T(8,128)(2,1)S(1)}, bf16[4,8,48,128]{3,2,1,0:T(8,128)(2,1)S(1)}, u32[]{:S(2)}, u32[]{:S(2)}) collective-permute-start(bf16[4,8,48,128]{3,2,1,0:T(8,128)(2,1)S(1)} %after.5.refs_2_), channel_id=1, source_target_pairs={{32,0},{33,1},{34,2},{35,3},{36,4},{37,5},{38,6},{39,7},{40,8},{41... | collective-permute-start | bytes 1179656 | tf_op jit(solution)/shard_map/ppermute | solution.py:453
  76.5 2.8 %outer.5.refs_1_ = f32[3072,128]{1,0:T(8,128)S(1)} custom-call(s32[8,4]{1,0:T(8,128)S(1)} %copy.40.columns, s32[3]{0:T(128)S(1)} %pad_add_fusion.refs_0_.flags, bf16[8,4,384,384]{3,2,1,0:T(8,128)(2,1)} %bitcast.83, f32[3072,128]{1,0:T(8,128)S(1)} %get-tuple-element.604.base, bf16[384,128]{1,0:T(8,128)(2,1)S(1)} %collective-permute-done.15.y_even.refs_1_, ...), custom_call_target="tpu_custom_call" | custom-call | flops 150994944 | bytes 6000000 | tf_op jit(solution)/shard_map/outer/pallas_call | solution.py:330
  79.3 2.6 %update.15 = (bf16[8,384,128]{2,1,0:T(8,128)(2,1)}, bf16[384,128]{1,0:T(8,128)(2,1)S(1)}, bf16[384,128]{1,0:T(8,128)(2,1)S(1)}, bf16[384,128]{1,0:T(8,128)(2,1)S...) custom-call(s32[3]{0:T(128)S(1)} %pad_add_fusion.refs_0_.flags, ...), custom_call_target="tpu_custom_call" | custom-call | tf_op jit(solution)/shard_map/update/pallas_call | solution.py:239
  82.0 2.1 %collective-permute-start.23 = (bf16[4,8,48,128]{3,2,1,0:T(8,128)(2,1)S(1)}, bf16[4,8,48,128]{3,2,1,0:T(8,128)(2,1)S(1)}, u32[]{:S(2)}, u32[]{:S(2)}) collective-permute-start(bf16[4,8,48,128]{3,2,1,0:T(8,128)(2,1)S(1)} %get-tuple-element.620), channel_id=1, source_target_pairs={{0,32},{32,0},{1,33},{33,1},{2,34},{34,2},{3,35},{35,3},{4,36},{36... | collective-permute-start | bytes 1179656 | tf_op jit(solution)/shard_map/ppermute | solution.py:448
  84.0 1.7 %collective-permute-done.23 = bf16[4,8,48,128]{3,2,1,0:T(8,128)(2,1)S(1)} collective-permute-done((bf16[4,8,48,128]{3,2,1,0:T(8,128)(2,1)S(1)}, bf16[4,8,48,128]{3,2,1,0:T(8,128)(2,1)S(1)}, u32[]{:S(2)}, u32[]{:S(2)}) %collective-permute-start.23) | collective-permute-done | bytes 393248 | tf_op jit(solution)/shard_map/ppermute | solution.py:448
  86.6 5.0 %all-to-all-start.5 = ((bf16[32,48,128]{2,1,0:T(8,128)(2,1)}), bf16[32,48,128]{2,1,0:T(8,128)(2,1)S(1)}, u32[]{:S(2)}, u32[]{:S(2)}) async-start(bf16[32,48,128]{2,1,0:T(8,128)(2,1)} %bitcast.27), calls=%async_computation.5 | async-start | bytes 786432 | tf_op jit(solution)/shard_map/all_to_all | solution.py:385
  91.6 2.7 %collective-permute-start.19 = (bf16[384,128]{1,0:T(8,128)(2,1)S(1)}, bf16[384,128]{1,0:T(8,128)(2,1)S(1)}, u32[]{:S(2)}, u32[]{:S(2)}) collective-permute-start(bf16[384,128]{1,0:T(8,128)(2,1)S(1)} %get-tuple-element.615), channel_id=1, source_target_pairs={{0,8},{8,0},{16,24},{24,16},{1,9},{9,1},{17,25},{25,17},{2,10},{10... | collective-permute-start | bytes 294920 | tf_op jit(solution)/shard_map/ppermute | solution.py:358
  97.0 6.1 %inner.12 = (f32[3072,128]{1,0:T(8,128)S(1)}, f32[8,128]{1,0:T(8,128)S(1)}) custom-call(s32[8,4]{1,0:T(8,128)S(1)} %copy.40.columns, s32[3]{0:T(128)S(1)} %pad_add_fusion.refs_0_.flags, bf16[8,4,384,384]{3,2,1,0:T(8,128)(2,1)} %bitcast.84, bf16[8,384,128]{2,1,0:T(8,128)(2,1)S(1)} %copy-done.3, bf16[384,128]{1,0:T(8,128)(2,1)S(1)} %collective-permute-done.19.x_even, ...), custom_call_target="tpu_custom_call" | custom-call | flops 1207959552 | bytes 12000000 | tf_op jit(solution)/shard_map/inner/pallas_call | solution.py:280
  103.7 1.6 %all-to-all-done.5 = bf16[32,48,128]{2,1,0:T(8,128)(2,1)S(1)} async-done(((bf16[32,48,128]{2,1,0:T(8,128)(2,1)}), bf16[32,48,128]{2,1,0:T(8,128)(2,1)S(1)}, u32[]{:S(2)}, u32[]{:S(2)}) %all-to-all-start.5) | async-done | bytes 393248 | tf_op jit(solution)/shard_map/all_to_all | solution.py:385
  105.3 4.0 %collective-permute-start.24 = (bf16[4,8,48,128]{3,2,1,0:T(8,128)(2,1)S(1)}, bf16[4,8,48,128]{3,2,1,0:T(8,128)(2,1)S(1)}, u32[]{:S(2)}, u32[]{:S(2)}) collective-permute-start(bf16[4,8,48,128]{3,2,1,0:T(8,128)(2,1)S(1)} %after.6.refs_2_), channel_id=1, source_target_pairs={{32,0},{33,1},{34,2},{35,3},{36,4},{37,5},{38,6},{39,7},{40,8},{41... | collective-permute-start | bytes 1179656 | tf_op jit(solution)/shard_map/ppermute | solution.py:453
  109.4 2.8 %outer.6.refs_1_ = f32[3072,128]{1,0:T(8,128)S(1)} custom-call(s32[8,4]{1,0:T(8,128)S(1)} %copy.40.columns, s32[3]{0:T(128)S(1)} %pad_add_fusion.refs_0_.flags, bf16[8,4,384,384]{3,2,1,0:T(8,128)(2,1)} %bitcast.85, f32[3072,128]{1,0:T(8,128)S(1)} %get-tuple-element.617.base, bf16[384,128]{1,0:T(8,128)(2,1)S(1)} %collective-permute-done.21.y_even.refs_1_, ...), custom_call_target="tpu_custom_call" | custom-call | flops 150994944 | bytes 6000000 | tf_op jit(solution)/shard_map/outer/pallas_call | solution.py:330
  112.3 2.3 %update.16 = (f32[3072,128]{1,0:T(8,128)}, f32[1,128]{1,0:T(1,128)S(1)}) custom-call(s32[3]{0:T(128)S(1)} %pad_add_fusion.refs_0_.flags, f32[3072,128]{1,0:T(8,128)S(1)} %outer.6.refs_1_, bf16[4,8,48,128]{3,2,1,0:T(8,128)(2,1)S(1)} %after.6.refs_2_, bf16[4,8,48,128]{3,2,1,0:T(8,128)(2,1)S(1)} %collective-permute-done.24.refs_3_, ...), custom_call_target="tpu_custom_call" | custom-call | tf_op jit(solution)/shard_map/update/pallas_call | solution.py:239
  114.6 13.6 %all_to_all.65 = f32[16,1,384]{2,1,0:T(1,128)S(1)} all-to-all(f32[16,1,384]{2,1,0:T(1,128)S(1)} %broadcast_in_dim.117), channel_id=1, replica_groups=mesh['zh'=4,'core'=2,'gx'=4,'y'=4,'zl'=2] {'gx','y'}, dimensions={0} | all-to-all | bytes 49152 | tf_op jit(solution)/shard_map/all_to_all | solution.py:369
  128.8 6.2 %all-to-all-start.7 = ((f32[16,1,384]{2,1,0:T(1,128)}), f32[16,1,384]{2,1,0:T(1,128)S(1)}, u32[]{:S(2)}, u32[]{:S(2)}) async-start(f32[16,1,384]{2,1,0:T(1,128)} %broadcast_in_dim.118), calls=%async_computation.7 | async-start | bytes 49152 | tf_op jit(solution)/shard_map/all_to_all | solution.py:369
  135.0 7.4 %all-to-all-done.7 = f32[16,1,384]{2,1,0:T(1,128)S(1)} async-done(((f32[16,1,384]{2,1,0:T(1,128)}), f32[16,1,384]{2,1,0:T(1,128)S(1)}, u32[]{:S(2)}, u32[]{:S(2)}) %all-to-all-start.7) | async-done | bytes 24608 | tf_op jit(solution)/shard_map/all_to_all | solution.py:369
  143.8 1.6 %conditional.1 = (f32[3,128]{1,0:T(4,128)S(1)}, f32[1,1,1,8,384,128]{5,4,3,2,1,0:T(8,128)S(1)}) conditional(s32[]{:T(128)} %convert_element_type.16, (s32[3]{0:T(128)S(1)}, f32[3072,128]{1,0:T(8,128)S(1)}, bf16[448,512]{1,0:T(8,128)(2,1)S(1)}, s32[]{:T(128)}, s32[8,4]{0,1:T(4,128)S(1)}, /*index=5*/bf16[8,4,384,384]{3,2,1,0:T(8,128)(2,1)}, ...), branch_computations={%region_3.9_spmd, %region_9.10_spmd} | conditional | flops 1359548672 | bytes 31461186 | solution.py:494
  143.9 1.5 %broadcast_multiply_fusion = f32[3072,128]{1,0:T(8,128)S(1)} fusion(f32[3072,128]{1,0:T(8,128)} %get-tuple-element.546, f32[128]{0:T(128)S(1)} %get-tuple-element.705), kind=kLoop, calls=%fused_computation.7 | loop fusion | flops 393216 | bytes 3146240 | tf_op jit(solution)/shard_map/cond/branch_1_fun/mul | solution.py:478
  (118 shorter events, 21.0 us)
Async XLA Ops:
  0.6 10.8 %copy-start.24 = (f32[1,8,7,1,8]{4,3,2,1,0:T(1,128)S(1)}, f32[1,8,7,1,8]{4,3,2,1,0:T(1,128)}, u32[]{:S(2)}) copy-start(f32[1,8,7,1,8]{4,3,2,1,0:T(1,128)} %param.17) | copy-start | bytes 5380
  5.9 18.1 %copy-start.27 = (s32[1,1,1,8,4]{3,4,2,1,0:T(4,128)S(1)}, s32[1,1,1,8,4]{3,4,2,1,0:T(4,128)}, u32[]{:S(2)}) copy-start(s32[1,1,1,8,4]{3,4,2,1,0:T(4,128)} %param.14) | copy-start | bytes 388
  5.9 18.2 %copy-start.1 = (bf16[8,384,128]{2,1,0:T(8,128)(2,1)S(1)}, bf16[8,384,128]{2,1,0:T(8,128)(2,1)}, u32[]{:S(2)}) copy-start(bf16[8,384,128]{2,1,0:T(8,128)(2,1)} %get-tuple-element.589.rounded) | copy-start | bytes 2359300
  5.9 6.9 %collective-permute-start.10 = (bf16[4,8,48,128]{3,2,1,0:T(8,128)(2,1)S(1)}, bf16[4,8,48,128]{3,2,1,0:T(8,128)(2,1)S(1)}, u32[]{:S(2)}, u32[]{:S(2)}) collective-permute-start(bf16[4,8,48,128]{3,2,1,0:T(8,128)(2,1)S(1)} %get-tuple-element.595), channel_id=1, source_target_pairs={{0,32},{32,0},{1,33},{33,1},{2,34},{34,2},{3,35},{35,3},{4,36},{36... | collective-permute-start | bytes 1179656 | tf_op jit(solution)/shard_map/ppermute | solution.py:448
  13.6 19.4 %all-to-all-start.3 = ((bf16[32,48,128]{2,1,0:T(8,128)(2,1)}), bf16[32,48,128]{2,1,0:T(8,128)(2,1)S(1)}, u32[]{:S(2)}, u32[]{:S(2)}) async-start(bf16[32,48,128]{2,1,0:T(8,128)(2,1)} %bitcast.22), calls=%async_computation.3 | async-start | bytes 786432 | tf_op jit(solution)/shard_map/all_to_all | solution.py:385
  20.1 4.0 %collective-permute-start.6 = (bf16[384,128]{1,0:T(8,128)(2,1)S(1)}, bf16[384,128]{1,0:T(8,128)(2,1)S(1)}, u32[]{:S(2)}, u32[]{:S(2)}) collective-permute-start(bf16[384,128]{1,0:T(8,128)(2,1)S(1)} %get-tuple-element.590), channel_id=1, source_target_pairs={{0,8},{8,0},{16,24},{24,16},{1,9},{9,1},{17,25},{25,17},{2,10},{10... | collective-permute-start | bytes 294920 | tf_op jit(solution)/shard_map/ppermute | solution.py:358
  21.4 2.7 %collective-permute-start.7 = (bf16[384,128]{1,0:T(8,128)(2,1)S(1)}, bf16[384,128]{1,0:T(8,128)(2,1)S(1)}, u32[]{:S(2)}, u32[]{:S(2)}) collective-permute-start(bf16[384,128]{1,0:T(8,128)(2,1)S(1)} %get-tuple-element.591), channel_id=1, source_target_pairs={{8,16},{16,8},{9,17},{17,9},{10,18},{18,10},{11,19},{19,11},{12,20... | collective-permute-start | bytes 294920 | tf_op jit(solution)/shard_map/ppermute | solution.py:359
  22.0 9.8 %collective-permute-start.8 = (bf16[384,128]{1,0:T(8,128)(2,1)}, bf16[384,128]{1,0:T(8,128)(2,1)S(1)}, u32[]{:S(2)}, u32[]{:S(2)}) collective-permute-start(bf16[384,128]{1,0:T(8,128)(2,1)} %get-tuple-element.593), channel_id=1, source_target_pairs={{0,1},{1,0},{2,3},{3,2},{4,5},{5,4},{6,7},{7,6},{8,9},{9,8},{10,11... | collective-permute-start | bytes 294920 | tf_op jit(solution)/shard_map/ppermute | solution.py:360
  23.4 8.5 %collective-permute-start.9 = (bf16[384,128]{1,0:T(8,128)(2,1)S(1)}, bf16[384,128]{1,0:T(8,128)(2,1)S(1)}, u32[]{:S(2)}, u32[]{:S(2)}) collective-permute-start(bf16[384,128]{1,0:T(8,128)(2,1)S(1)} %get-tuple-element.594), channel_id=1, source_target_pairs={{1,2},{2,1},{3,4},{4,3},{5,6},{6,5},{9,10},{10,9},{11,12},{12,11},... | collective-permute-start | bytes 294920 | tf_op jit(solution)/shard_map/ppermute | solution.py:361
  33.1 9.7 %collective-permute-start.11 = (bf16[4,8,48,128]{3,2,1,0:T(8,128)(2,1)S(1)}, bf16[4,8,48,128]{3,2,1,0:T(8,128)(2,1)S(1)}, u32[]{:S(2)}, u32[]{:S(2)}) collective-permute-start(bf16[4,8,48,128]{3,2,1,0:T(8,128)(2,1)S(1)} %after.4.refs_2_), channel_id=1, source_target_pairs={{32,0},{33,1},{34,2},{35,3},{36,4},{37,5},{38,6},{39,7},{40,8},{41... | collective-permute-start | bytes 1179656 | tf_op jit(solution)/shard_map/ppermute | solution.py:453
  38.2 4.6 %collective-permute-start.12 = (bf16[8,48,128]{2,1,0:T(8,128)(2,1)S(1)}, bf16[8,48,128]{2,1,0:T(8,128)(2,1)S(1)}, u32[]{:S(2)}, u32[]{:S(2)}) collective-permute-start(bf16[8,48,128]{2,1,0:T(8,128)(2,1)S(1)} %slice_bitcast_fusion), channel_id=1, source_target_pairs={{64,0},{65,1},{66,2},{67,3},{68,4},{69,5},{70,6},{71,7},{72,8},{73... | collective-permute-start | bytes 294920 | tf_op jit(solution)/shard_map/ppermute | solution.py:459
  46.2 16.8 %copy-start.2 = (bf16[8,384,128]{2,1,0:T(8,128)(2,1)S(1)}, bf16[8,384,128]{2,1,0:T(8,128)(2,1)}, u32[]{:S(2)}) copy-start(bf16[8,384,128]{2,1,0:T(8,128)(2,1)} %get-tuple-element.601.rounded) | copy-start | bytes 2359300
  46.2 7.1 %collective-permute-start.17 = (bf16[4,8,48,128]{3,2,1,0:T(8,128)(2,1)S(1)}, bf16[4,8,48,128]{3,2,1,0:T(8,128)(2,1)S(1)}, u32[]{:S(2)}, u32[]{:S(2)}) collective-permute-start(bf16[4,8,48,128]{3,2,1,0:T(8,128)(2,1)S(1)} %get-tuple-element.607), channel_id=1, source_target_pairs={{0,32},{32,0},{1,33},{33,1},{2,34},{34,2},{3,35},{35,3},{4,36},{36... | collective-permute-start | bytes 1179656 | tf_op jit(solution)/shard_map/ppermute | solution.py:448
  54.1 17.4 %all-to-all-start.4 = ((bf16[32,48,128]{2,1,0:T(8,128)(2,1)}), bf16[32,48,128]{2,1,0:T(8,128)(2,1)S(1)}, u32[]{:S(2)}, u32[]{:S(2)}) async-start(bf16[32,48,128]{2,1,0:T(8,128)(2,1)} %bitcast.25), calls=%async_computation.4 | async-start | bytes 786432 | tf_op jit(solution)/shard_map/all_to_all | solution.py:385
  58.4 4.5 %collective-permute-start.13 = (bf16[384,128]{1,0:T(8,128)(2,1)S(1)}, bf16[384,128]{1,0:T(8,128)(2,1)S(1)}, u32[]{:S(2)}, u32[]{:S(2)}) collective-permute-start(bf16[384,128]{1,0:T(8,128)(2,1)S(1)} %get-tuple-element.602), channel_id=1, source_target_pairs={{0,8},{8,0},{16,24},{24,16},{1,9},{9,1},{17,25},{25,17},{2,10},{10... | collective-permute-start | bytes 294920 | tf_op jit(solution)/shard_map/ppermute | solution.py:358
  60.3 2.7 %collective-permute-start.14 = (bf16[384,128]{1,0:T(8,128)(2,1)S(1)}, bf16[384,128]{1,0:T(8,128)(2,1)S(1)}, u32[]{:S(2)}, u32[]{:S(2)}) collective-permute-start(bf16[384,128]{1,0:T(8,128)(2,1)S(1)} %get-tuple-element.603), channel_id=1, source_target_pairs={{8,16},{16,8},{9,17},{17,9},{10,18},{18,10},{11,19},{19,11},{12,20... | collective-permute-start | bytes 294920 | tf_op jit(solution)/shard_map/ppermute | solution.py:359
  61.0 9.3 %collective-permute-start.15 = (bf16[384,128]{1,0:T(8,128)(2,1)}, bf16[384,128]{1,0:T(8,128)(2,1)S(1)}, u32[]{:S(2)}, u32[]{:S(2)}) collective-permute-start(bf16[384,128]{1,0:T(8,128)(2,1)} %get-tuple-element.605), channel_id=1, source_target_pairs={{0,1},{1,0},{2,3},{3,2},{4,5},{5,4},{6,7},{7,6},{8,9},{9,8},{10,11... | collective-permute-start | bytes 294920 | tf_op jit(solution)/shard_map/ppermute | solution.py:360
  62.3 8.0 %collective-permute-start.16 = (bf16[384,128]{1,0:T(8,128)(2,1)S(1)}, bf16[384,128]{1,0:T(8,128)(2,1)S(1)}, u32[]{:S(2)}, u32[]{:S(2)}) collective-permute-start(bf16[384,128]{1,0:T(8,128)(2,1)S(1)} %get-tuple-element.606), channel_id=1, source_target_pairs={{1,2},{2,1},{3,4},{4,3},{5,6},{6,5},{9,10},{10,9},{11,12},{12,11},... | collective-permute-start | bytes 294920 | tf_op jit(solution)/shard_map/ppermute | solution.py:361
  71.6 7.7 %collective-permute-start.18 = (bf16[4,8,48,128]{3,2,1,0:T(8,128)(2,1)S(1)}, bf16[4,8,48,128]{3,2,1,0:T(8,128)(2,1)S(1)}, u32[]{:S(2)}, u32[]{:S(2)}) collective-permute-start(bf16[4,8,48,128]{3,2,1,0:T(8,128)(2,1)S(1)} %after.5.refs_2_), channel_id=1, source_target_pairs={{32,0},{33,1},{34,2},{35,3},{36,4},{37,5},{38,6},{39,7},{40,8},{41... | collective-permute-start | bytes 1179656 | tf_op jit(solution)/shard_map/ppermute | solution.py:453
  82.0 15.0 %copy-start.3 = (bf16[8,384,128]{2,1,0:T(8,128)(2,1)S(1)}, bf16[8,384,128]{2,1,0:T(8,128)(2,1)}, u32[]{:S(2)}) copy-start(bf16[8,384,128]{2,1,0:T(8,128)(2,1)} %get-tuple-element.614.rounded) | copy-start | bytes 2359300
  82.0 3.7 %collective-permute-start.23 = (bf16[4,8,48,128]{3,2,1,0:T(8,128)(2,1)S(1)}, bf16[4,8,48,128]{3,2,1,0:T(8,128)(2,1)S(1)}, u32[]{:S(2)}, u32[]{:S(2)}) collective-permute-start(bf16[4,8,48,128]{3,2,1,0:T(8,128)(2,1)S(1)} %get-tuple-element.620), channel_id=1, source_target_pairs={{0,32},{32,0},{1,33},{33,1},{2,34},{34,2},{3,35},{35,3},{4,36},{36... | collective-permute-start | bytes 1179656 | tf_op jit(solution)/shard_map/ppermute | solution.py:448
  86.6 18.7 %all-to-all-start.5 = ((bf16[32,48,128]{2,1,0:T(8,128)(2,1)}), bf16[32,48,128]{2,1,0:T(8,128)(2,1)S(1)}, u32[]{:S(2)}, u32[]{:S(2)}) async-start(bf16[32,48,128]{2,1,0:T(8,128)(2,1)} %bitcast.27), calls=%async_computation.5 | async-start | bytes 786432 | tf_op jit(solution)/shard_map/all_to_all | solution.py:385
  91.6 5.3 %collective-permute-start.19 = (bf16[384,128]{1,0:T(8,128)(2,1)S(1)}, bf16[384,128]{1,0:T(8,128)(2,1)S(1)}, u32[]{:S(2)}, u32[]{:S(2)}) collective-permute-start(bf16[384,128]{1,0:T(8,128)(2,1)S(1)} %get-tuple-element.615), channel_id=1, source_target_pairs={{0,8},{8,0},{16,24},{24,16},{1,9},{9,1},{17,25},{25,17},{2,10},{10... | collective-permute-start | bytes 294920 | tf_op jit(solution)/shard_map/ppermute | solution.py:358
  94.3 2.7 %collective-permute-start.20 = (bf16[384,128]{1,0:T(8,128)(2,1)S(1)}, bf16[384,128]{1,0:T(8,128)(2,1)S(1)}, u32[]{:S(2)}, u32[]{:S(2)}) collective-permute-start(bf16[384,128]{1,0:T(8,128)(2,1)S(1)} %get-tuple-element.616), channel_id=1, source_target_pairs={{8,16},{16,8},{9,17},{17,9},{10,18},{18,10},{11,19},{19,11},{12,20... | collective-permute-start | bytes 294920 | tf_op jit(solution)/shard_map/ppermute | solution.py:359
  95.0 8.7 %collective-permute-start.21 = (bf16[384,128]{1,0:T(8,128)(2,1)S(1)}, bf16[384,128]{1,0:T(8,128)(2,1)S(1)}, u32[]{:S(2)}, u32[]{:S(2)}) collective-permute-start(bf16[384,128]{1,0:T(8,128)(2,1)S(1)} %get-tuple-element.618), channel_id=1, source_target_pairs={{0,1},{1,0},{2,3},{3,2},{4,5},{5,4},{6,7},{7,6},{8,9},{9,8},{10,11... | collective-permute-start | bytes 294920 | tf_op jit(solution)/shard_map/ppermute | solution.py:360
  96.3 7.4 %collective-permute-start.22 = (bf16[384,128]{1,0:T(8,128)(2,1)S(1)}, bf16[384,128]{1,0:T(8,128)(2,1)S(1)}, u32[]{:S(2)}, u32[]{:S(2)}) collective-permute-start(bf16[384,128]{1,0:T(8,128)(2,1)S(1)} %get-tuple-element.619), channel_id=1, source_target_pairs={{1,2},{2,1},{3,4},{4,3},{5,6},{6,5},{9,10},{10,9},{11,12},{12,11},... | collective-permute-start | bytes 294920 | tf_op jit(solution)/shard_map/ppermute | solution.py:361
  105.3 6.8 %collective-permute-start.24 = (bf16[4,8,48,128]{3,2,1,0:T(8,128)(2,1)S(1)}, bf16[4,8,48,128]{3,2,1,0:T(8,128)(2,1)S(1)}, u32[]{:S(2)}, u32[]{:S(2)}) collective-permute-start(bf16[4,8,48,128]{3,2,1,0:T(8,128)(2,1)S(1)} %after.6.refs_2_), channel_id=1, source_target_pairs={{32,0},{33,1},{34,2},{35,3},{36,4},{37,5},{38,6},{39,7},{40,8},{41... | collective-permute-start | bytes 1179656 | tf_op jit(solution)/shard_map/ppermute | solution.py:453
  112.2 31.5 %copy-start.13 = (bf16[448,512]{1,0:T(8,128)(2,1)S(1)}, bf16[448,512]{1,0:T(8,128)(2,1)}, u32[]{:S(2)}) copy-start(bf16[448,512]{1,0:T(8,128)(2,1)} %copy-done.10) | copy-start | bytes 1376260
  112.3 31.5 %copy-start.17 = (bf16[512,448]{1,0:T(8,128)(2,1)S(1)}, bf16[512,448]{1,0:T(8,128)(2,1)}, u32[]{:S(2)}) copy-start(bf16[512,448]{1,0:T(8,128)(2,1)} %fusion.refs_7_) | copy-start | bytes 1376260
  112.3 31.5 %copy-start.20 = (f32[448,128]{1,0:T(8,128)S(1)}, f32[448,128]{1,0:T(8,128)}, u32[]{:S(2)}) copy-start(f32[448,128]{1,0:T(8,128)} %get-tuple-element.612.refs_6_) | copy-start | bytes 688132
  112.3 31.5 %copy-start.22 = (f32[1,1,1,8,384,128]{5,4,3,2,1,0:T(8,128)S(1)}, f32[1,1,1,8,384,128]{5,4,3,2,1,0:T(8,128)}, u32[]{:S(2)}) copy-start(f32[1,1,1,8,384,128]{5,4,3,2,1,0:T(8,128)} %param.12) | copy-start | bytes 4718596
  128.8 13.6 %all-to-all-start.7 = ((f32[16,1,384]{2,1,0:T(1,128)}), f32[16,1,384]{2,1,0:T(1,128)S(1)}, u32[]{:S(2)}, u32[]{:S(2)}) async-start(f32[16,1,384]{2,1,0:T(1,128)} %broadcast_in_dim.118), calls=%async_computation.7 | async-start | bytes 49152 | tf_op jit(solution)/shard_map/all_to_all | solution.py:369
  (17 other events, 41.5 us)
